TPU v7x, 32 devices: a whole 2x2x4 slice. The times are simulated.
32 devices in a mesh: section: 4 (over y, x), row: 4 (over z), col: 2 (over core).
Axes of the slice: x: 2, y: 2, z: 4, core: 2. Of those that a mesh axis runs over, the one named last changes fastest.
Arguments:
- hidden: bfloat16 [4, 256, 2, 3072], P(None, ('row', 'col')), may hold values from -6 to 6
- patch_counts: int32 [2, 4], replicated, may hold values from 128 to 256, as said below
- timestep: int32 [1], replicated, may hold values from 0 to 999
- time_table: float32 [1000, 512], replicated, may hold values from -6 to 6
- ada_weight: bfloat16 [4, 512, 18432], P('section', None, ('row', 'col')), may hold values from -0.25 to 0.25
- qkv_weight: bfloat16 [4, 3072, 9216], P('section', None, 'col'), may hold values from -0.109375 to 0.109375
- out_weight: bfloat16 [4, 3072, 3072], P('section', 'col'), may hold values from -0.109375 to 0.109375
- qk_gain: float32 [4, 2, 64], P('section'), may hold values from 1 to 3
- stale_kv: bfloat16 [4, 1024, 2, 48, 128], P('section', None, None, 'col'), may hold values from -8 to 8
- stale_inputs: bfloat16 [4, 96, 2, 3072], P('section', ('row', 'col')), may hold values from -6 to 6
- recompute_slots: int32 [2, 96], replicated, may hold values from 0 to 1023, as said below
Outputs:
- layer_outputs: bfloat16 [4, 4, 256, 2, 3072], P('section', None, ('row', 'col'))
Inputs may be any that keep to these rules, and one draw needn't show every extreme that they name: `patch_counts`: in every request one patch holds exactly 256 live tokens and another exactly 128. `recompute_slots`: the slots of one request are distinct.
All inputs are finite; a program needn't handle non-finite values.
Results may differ from a plain program's by a relative error of at most 0.035.
Values may be sent and summed in bfloat16 or wider, within the bound.
A program may use at most 192 MiB of HBM per device.

v0:
```python
import jax
import jax.numpy as jnp
from jax import lax
from jax.sharding import PartitionSpec as P

HD = 64
TXT = 226
GH = 30
GW = 45
PLEN = 256


def passed_along(value, axis, by):
    size = lax.axis_size(axis)
    pairs = [(i, i + by) for i in range(size) if 0 <= i + by < size]
    return lax.ppermute(value, axis, pairs)


def layer_norm(values, epsilon):
    centered = values - jnp.mean(values, axis=-1, keepdims=True)
    return centered * lax.rsqrt(jnp.mean(centered * centered, axis=-1, keepdims=True) + epsilon)


def rotary_tables(positions):
    video_index = jnp.maximum(positions - TXT, 0)
    is_video = positions >= TXT
    frame_index = video_index // (GH * GW)
    height_index = video_index // GW % GH
    width_index = video_index % GW
    phase_parts = []
    for coordinate, part_size in (
        (frame_index, HD // 4),
        (height_index, HD * 3 // 8),
        (width_index, HD * 3 // 8),
    ):
        frequency = 1.0 / 10000.0 ** (jnp.arange(0, part_size, 2).astype(jnp.float32) / part_size)
        phase_part = coordinate.astype(jnp.float32)[..., None] * frequency
        phase_parts.append(jnp.repeat(phase_part, 2, axis=-1))
    phase_all = jnp.concatenate(phase_parts, axis=-1)
    cosine = jnp.where(is_video[..., None], jnp.cos(phase_all), 1.0)
    sine_table = jnp.where(is_video[..., None], jnp.sin(phase_all), 0.0)
    return (cosine, sine_table)


def rotate_pairs(values, cosine, sine_table):
    paired = values.reshape(values.shape[:-1] + (values.shape[-1] // 2, 2))
    turned = jnp.stack([-paired[..., 1], paired[..., 0]], axis=-1).reshape(values.shape)
    return values * cosine + turned * sine_table


def heads_from(mixed_rows, positions, gain_pair):
    cosine, sine_table = rotary_tables(positions)
    cosine = cosine[..., None, :]
    sine_table = sine_table[..., None, :]
    keys_new = rotate_pairs(
        layer_norm(mixed_rows[..., 1, :], 1e-06) * gain_pair[1], cosine, sine_table
    ).astype(jnp.bfloat16)
    values_new = mixed_rows[..., 2, :].astype(jnp.bfloat16)
    queries = rotate_pairs(
        layer_norm(mixed_rows[..., 0, :], 1e-06) * gain_pair[0], cosine, sine_table
    ).astype(jnp.bfloat16)
    return jnp.concatenate([queries, keys_new, values_new], axis=-1)


def modulate(row_values, positions, modulation):
    is_text = (positions < TXT)[..., None]
    shifts = jnp.where(is_text, modulation[3], modulation[0])
    scales = jnp.where(is_text, modulation[4], modulation[1])
    normed = layer_norm(row_values.astype(jnp.float32), 1e-05)
    return (normed * (1.0 + scales) + shifts).astype(jnp.bfloat16)


def local(
    hidden,
    patch_counts,
    timestep,
    time_table,
    ada_weight,
    qkv_weight,
    out_weight,
    qk_gain,
    stale_kv,
    stale_inputs,
    recompute_slots,
):
    col_count = lax.axis_size("col")
    section_count = lax.axis_size("section")
    section_index = lax.axis_index("section")
    row_index = lax.axis_index("row")
    col_index = lax.axis_index("col")
    num_patches, dev_rows, num_requests, model_width = hidden.shape
    seq_length = PLEN * num_patches
    group_rows = dev_rows * col_count
    starts = jnp.cumsum(patch_counts, axis=1) - patch_counts
    slot_index = jnp.arange(seq_length, dtype=jnp.int32)
    slot_patch = slot_index // PLEN
    slot_offset = slot_index % PLEN
    positions = starts[:, slot_patch] + slot_offset[None, :]
    live_mask = slot_offset[None, :] < patch_counts[:, slot_patch]
    embedding = jax.nn.silu(time_table[timestep[0]]).astype(jnp.bfloat16)
    mod_part = jnp.dot(embedding, ada_weight[0], preferred_element_type=jnp.float32)
    modulation = lax.all_gather(mod_part, ("row", "col"), axis=0, tiled=True).reshape(
        6, model_width
    )
    weights_qkv = qkv_weight[0]
    weights_out = out_weight[0]
    gain_pair = qk_gain[0]
    scale_factor = HD ** (-0.5)

    def project(normed_part, position_table):
        piece_rows = lax.all_gather(normed_part, "col", axis=0, tiled=True)
        mixed_rows = jnp.dot(
            piece_rows.reshape(-1, model_width), weights_qkv, preferred_element_type=jnp.float32
        )
        mixed_rows = mixed_rows.reshape(piece_rows.shape[0], piece_rows.shape[1], -1, 3, HD)
        return heads_from(mixed_rows, position_table, gain_pair)

    def spread_rows(key_value):
        return lax.all_gather(key_value, "row", axis=0, tiled=True)

    rec_dev = stale_inputs.shape[1]
    rec_group = rec_dev * col_count
    rec_positions = jnp.take_along_axis(positions, recompute_slots, axis=1).T
    local_rec = lax.dynamic_slice_in_dim(
        rec_positions, (row_index * col_count + col_index) * rec_dev, rec_dev, 0
    )
    group_rec = lax.dynamic_slice_in_dim(rec_positions, row_index * rec_group, rec_group, 0)
    rec_normed = modulate(stale_inputs[0], local_rec, modulation)
    rec_heads = project(rec_normed, group_rec)
    rec_pairs = spread_rows(rec_heads[..., HD:])
    base_cache = stale_kv[0]
    for request in range(num_requests):
        base_cache = base_cache.at[recompute_slots[request], request].set(rec_pairs[:, request])
    batches = num_requests * num_patches // num_requests
    turn_count = batches + section_count - 1
    local_offsets = (
        row_index * group_rows + col_index * dev_rows + jnp.arange(dev_rows, dtype=jnp.int32)
    )
    group_offsets = row_index * group_rows + jnp.arange(group_rows, dtype=jnp.int32)

    def relay_turn(turn_index, loop_state):
        cache_table, outputs, incoming = loop_state
        batch_index = turn_index - section_index
        is_valid = (batch_index >= 0) & (batch_index < batches)
        clipped = jnp.clip(batch_index, 0, batches - 1)
        first_request = clipped // num_patches * num_requests
        patch_index = clipped % num_patches
        request_starts = starts[:, patch_index]
        local_positions = local_offsets[:, None] + request_starts[None, :]
        group_positions = group_offsets[:, None] + request_starts[None, :]
        entering = hidden[patch_index]
        inputs = jnp.where(section_index == 0, entering, incoming)
        normed = modulate(inputs, local_positions, modulation)
        heads_all = project(normed, group_positions)
        fresh_pairs = spread_rows(heads_all[..., HD:])
        block_start = (patch_index * PLEN, first_request, 0, 0)
        old_block = lax.dynamic_slice(cache_table, block_start, fresh_pairs.shape)
        new_block = jnp.where(is_valid, fresh_pairs, old_block)
        cache_table = lax.dynamic_update_slice(cache_table, new_block, block_start)
        queries = heads_all[..., :HD]
        scores = (
            jnp.einsum(
                "qrhd,krhd->rhqk",
                queries,
                cache_table[..., :HD],
                preferred_element_type=jnp.float32,
            )
            * scale_factor
        )
        weights = jnp.where(live_mask[:, None, None, :], jnp.exp(scores), 0.0)
        totals = jnp.sum(weights, axis=-1)
        attended = jnp.einsum(
            "rhqk,krhd->qrhd",
            weights.astype(jnp.bfloat16),
            cache_table[..., HD:],
            preferred_element_type=jnp.float32,
        )
        attended = (attended / jnp.transpose(totals, (2, 0, 1))[..., None]).astype(jnp.bfloat16)
        flat_rows = attended.reshape(group_rows * num_requests, -1)
        projected = (
            lax.psum_scatter(
                jnp.dot(flat_rows, weights_out, preferred_element_type=jnp.float32).astype(
                    jnp.bfloat16
                ),
                "col",
                scatter_dimension=0,
                tiled=True,
            )
            .astype(jnp.float32)
            .reshape(dev_rows, num_requests, model_width)
        )
        is_text = (local_positions < TXT)[..., None]
        gate_rows = jnp.where(is_text, modulation[5], modulation[2])
        leaving = (inputs.astype(jnp.float32) + gate_rows * projected).astype(jnp.bfloat16)
        out_start = (patch_index, 0, first_request, 0)
        current_out = lax.dynamic_slice(
            outputs, out_start, (1, dev_rows, num_requests, model_width)
        )
        written = jnp.where(is_valid, leaving[None], current_out)
        outputs = lax.dynamic_update_slice(outputs, written, out_start)
        incoming = passed_along(leaving, "section", 1)
        return (cache_table, outputs, incoming)

    outputs_start = jnp.zeros((num_patches, dev_rows, num_requests, model_width), jnp.bfloat16)
    incoming_start = jnp.zeros((dev_rows, num_requests, model_width), jnp.bfloat16)
    final_state = lax.fori_loop(
        0, turn_count, relay_turn, (base_cache, outputs_start, incoming_start)
    )
    return final_state[1][None]


def solution(mesh):
    return jax.shard_map(
        local,
        mesh=mesh,
        in_specs=(
            P(None, ("row", "col"), None, None),
            P(),
            P(),
            P(),
            P("section", None, ("row", "col")),
            P("section", None, "col"),
            P("section", "col", None),
            P("section", None, None),
            P("section", None, None, "col", None),
            P("section", ("row", "col"), None, None),
            P(),
        ),
        out_specs=P("section", None, ("row", "col"), None, None),
        check_vma=False,
    )
```

profile of v0, /device:TPU:6, one launch (start us, length us, event | category | flops | bytes accessed | tf_op | source)
XLA Modules:
  0.0 1408.2 jit_solution(1260628717219506568)
XLA Ops:
  42.2 36.7 %copy.74 = bf16[1,3072,4608]{1,2,0:T(8,128)(2,1)} copy(bf16[1,3072,4608]{2,1,0:T(8,128)(2,1)} %param.18) | data formatting | bytes 56623104 | tf_op args[5]
  78.9 17.4 %fusion.51 = f32[24,2,24,3,64]{4,0,3,2,1:T(8,128)S(1)} fusion(bf16[24,3,64,3072,1]{3,2,1,0,4:T(8,128)(2,1)} %bitcast.241, bf16[24,2,3072,1,1]{2,1,0,4,3:T(2,128)(2,1)S(1)} %bitcast.256), kind=kOutput, calls=%fused_computation.125 | convolution fusion | flops 1358954496 | bytes 29491200 | tf_op jit(solution)/shard_map/dot_general | solution.py:112
  110.7 27.2 %all-gather.4.cloned.1.call-done = bf16[96,2,24,128]{3,0,2,1:T(8,128)(2,1)} async-done(((bf16[24,2,24,128]{3,0,2,1:T(8,128)(2,1)}), bf16[96,2,24,128]{3,0,2,1:T(8,128)(2,1)}) %all-gather.4.cloned.1.call-update) | async-done | bytes 1179664 | tf_op jit(solution)/shard_map/all_gather | solution.py:119
  178.4 1221.5 %while.21 = (s32[]{:T(128)}, bf16[1024,2,24,128]{3,0,2,1:T(8,128)(2,1)}, bf16[4,32,2,3072]{3,2,1,0:T(2,128)(2,1)}, bf16[32,2,3072]{2,0,1:T(8,128)(2,1)S(1)}, s32...) while((s32[]{:T(128)}, ...), condition=%wide.region_16.17_spmd.clone, body=%wide.region_7.16_spmd.clone.sunk | while | flops 5670415360 | bytes 222939120 | solution.py:206
  185.0 17.2 %fusion.111 = f32[64,2,24,3,64]{4,0,3,2,1:T(8,128)S(1)} fusion(bf16[24,3,64,3072,1]{3,2,1,0,4:T(8,128)(2,1)} %bitcast.243, bf16[64,2,3072]{2,0,1:T(8,128)(2,1)S(1)} %all_gather.38), kind=kOutput, calls=%fused_computation.46.clone.1 | convolution fusion | flops 3623878656 | bytes 31457280 | tf_op jit(solution)/shard_map/while/body/eval_jaxpr/dot_general | solution.py:112
  225.5 16.8 %copy.142 = bf16[1024,2,24,128]{0,3,2,1:T(8,128)(2,1)} copy(bf16[1024,2,24,128]{3,0,2,1:T(8,128)(2,1)} %get-tuple-element.780) | data formatting | bytes 25165824 | tf_op jit(solution)/shard_map/while
  242.3 39.7 %all-gather.6.cloned.1.call-done = bf16[256,2,24,128]{3,0,2,1:T(8,128)(2,1)} async-done(((bf16[64,2,24,128]{3,0,2,1:T(8,128)(2,1)}), bf16[256,2,24,128]{3,0,2,1:T(8,128)(2,1)}) %all-gather.6.cloned.1.call-update) | async-done | bytes 3145744 | tf_op jit(solution)/shard_map/while/body/eval_jaxpr/all_gather | solution.py:119
  359.3 17.2 %fusion.111 = f32[64,2,24,3,64]{4,0,3,2,1:T(8,128)S(1)} fusion(bf16[24,3,64,3072,1]{3,2,1,0,4:T(8,128)(2,1)} %bitcast.243, bf16[64,2,3072]{2,0,1:T(8,128)(2,1)S(1)} %all_gather.38), kind=kOutput, calls=%fused_computation.46.clone.1 | convolution fusion | flops 3623878656 | bytes 31457280 | tf_op jit(solution)/shard_map/while/body/eval_jaxpr/dot_general | solution.py:112
  399.8 16.8 %copy.142 = bf16[1024,2,24,128]{0,3,2,1:T(8,128)(2,1)} copy(bf16[1024,2,24,128]{3,0,2,1:T(8,128)(2,1)} %get-tuple-element.780) | data formatting | bytes 25165824 | tf_op jit(solution)/shard_map/while
  416.6 39.1 %all-gather.6.cloned.1.call-done = bf16[256,2,24,128]{3,0,2,1:T(8,128)(2,1)} async-done(((bf16[64,2,24,128]{3,0,2,1:T(8,128)(2,1)}), bf16[256,2,24,128]{3,0,2,1:T(8,128)(2,1)}) %all-gather.6.cloned.1.call-update) | async-done | bytes 3145744 | tf_op jit(solution)/shard_map/while/body/eval_jaxpr/all_gather | solution.py:119
  532.9 17.2 %fusion.111 = f32[64,2,24,3,64]{4,0,3,2,1:T(8,128)S(1)} fusion(bf16[24,3,64,3072,1]{3,2,1,0,4:T(8,128)(2,1)} %bitcast.243, bf16[64,2,3072]{2,0,1:T(8,128)(2,1)S(1)} %all_gather.38), kind=kOutput, calls=%fused_computation.46.clone.1 | convolution fusion | flops 3623878656 | bytes 31457280 | tf_op jit(solution)/shard_map/while/body/eval_jaxpr/dot_general | solution.py:112
  573.4 16.8 %copy.142 = bf16[1024,2,24,128]{0,3,2,1:T(8,128)(2,1)} copy(bf16[1024,2,24,128]{3,0,2,1:T(8,128)(2,1)} %get-tuple-element.780) | data formatting | bytes 25165824 | tf_op jit(solution)/shard_map/while
  590.2 39.1 %all-gather.6.cloned.1.call-done = bf16[256,2,24,128]{3,0,2,1:T(8,128)(2,1)} async-done(((bf16[64,2,24,128]{3,0,2,1:T(8,128)(2,1)}), bf16[256,2,24,128]{3,0,2,1:T(8,128)(2,1)}) %all-gather.6.cloned.1.call-update) | async-done | bytes 3145744 | tf_op jit(solution)/shard_map/while/body/eval_jaxpr/all_gather | solution.py:119
  706.6 17.2 %fusion.111 = f32[64,2,24,3,64]{4,0,3,2,1:T(8,128)S(1)} fusion(bf16[24,3,64,3072,1]{3,2,1,0,4:T(8,128)(2,1)} %bitcast.243, bf16[64,2,3072]{2,0,1:T(8,128)(2,1)S(1)} %all_gather.38), kind=kOutput, calls=%fused_computation.46.clone.1 | convolution fusion | flops 3623878656 | bytes 31457280 | tf_op jit(solution)/shard_map/while/body/eval_jaxpr/dot_general | solution.py:112
  763.8 40.0 %all-gather.6.cloned.1.call-done = bf16[256,2,24,128]{3,0,2,1:T(8,128)(2,1)} async-done(((bf16[64,2,24,128]{3,0,2,1:T(8,128)(2,1)}), bf16[256,2,24,128]{3,0,2,1:T(8,128)(2,1)}) %all-gather.6.cloned.1.call-update) | async-done | bytes 3145744 | tf_op jit(solution)/shard_map/while/body/eval_jaxpr/all_gather | solution.py:119
  882.1 17.2 %fusion.111 = f32[64,2,24,3,64]{4,0,3,2,1:T(8,128)S(1)} fusion(bf16[24,3,64,3072,1]{3,2,1,0,4:T(8,128)(2,1)} %bitcast.243, bf16[64,2,3072]{2,0,1:T(8,128)(2,1)S(1)} %all_gather.38), kind=kOutput, calls=%fused_computation.46.clone.1 | convolution fusion | flops 3623878656 | bytes 31457280 | tf_op jit(solution)/shard_map/while/body/eval_jaxpr/dot_general | solution.py:112
  922.6 16.8 %copy.142 = bf16[1024,2,24,128]{0,3,2,1:T(8,128)(2,1)} copy(bf16[1024,2,24,128]{3,0,2,1:T(8,128)(2,1)} %get-tuple-element.780) | data formatting | bytes 25165824 | tf_op jit(solution)/shard_map/while
  939.4 39.2 %all-gather.6.cloned.1.call-done = bf16[256,2,24,128]{3,0,2,1:T(8,128)(2,1)} async-done(((bf16[64,2,24,128]{3,0,2,1:T(8,128)(2,1)}), bf16[256,2,24,128]{3,0,2,1:T(8,128)(2,1)}) %all-gather.6.cloned.1.call-update) | async-done | bytes 3145744 | tf_op jit(solution)/shard_map/while/body/eval_jaxpr/all_gather | solution.py:119
  1056.9 17.3 %fusion.111 = f32[64,2,24,3,64]{4,0,3,2,1:T(8,128)S(1)} fusion(bf16[24,3,64,3072,1]{3,2,1,0,4:T(8,128)(2,1)} %bitcast.243, bf16[64,2,3072]{2,0,1:T(8,128)(2,1)S(1)} %all_gather.38), kind=kOutput, calls=%fused_computation.46.clone.1 | convolution fusion | flops 3623878656 | bytes 31457280 | tf_op jit(solution)/shard_map/while/body/eval_jaxpr/dot_general | solution.py:112
  1097.4 16.8 %copy.142 = bf16[1024,2,24,128]{0,3,2,1:T(8,128)(2,1)} copy(bf16[1024,2,24,128]{3,0,2,1:T(8,128)(2,1)} %get-tuple-element.780) | data formatting | bytes 25165824 | tf_op jit(solution)/shard_map/while
  1114.2 39.1 %all-gather.6.cloned.1.call-done = bf16[256,2,24,128]{3,0,2,1:T(8,128)(2,1)} async-done(((bf16[64,2,24,128]{3,0,2,1:T(8,128)(2,1)}), bf16[256,2,24,128]{3,0,2,1:T(8,128)(2,1)}) %all-gather.6.cloned.1.call-update) | async-done | bytes 3145744 | tf_op jit(solution)/shard_map/while/body/eval_jaxpr/all_gather | solution.py:119
  1231.6 17.3 %fusion.111 = f32[64,2,24,3,64]{4,0,3,2,1:T(8,128)S(1)} fusion(bf16[24,3,64,3072,1]{3,2,1,0,4:T(8,128)(2,1)} %bitcast.243, bf16[64,2,3072]{2,0,1:T(8,128)(2,1)S(1)} %all_gather.38), kind=kOutput, calls=%fused_computation.46.clone.1 | convolution fusion | flops 3623878656 | bytes 31457280 | tf_op jit(solution)/shard_map/while/body/eval_jaxpr/dot_general | solution.py:112
  1272.1 16.8 %copy.142 = bf16[1024,2,24,128]{0,3,2,1:T(8,128)(2,1)} copy(bf16[1024,2,24,128]{3,0,2,1:T(8,128)(2,1)} %get-tuple-element.780) | data formatting | bytes 25165824 | tf_op jit(solution)/shard_map/while
  1288.8 39.1 %all-gather.6.cloned.1.call-done = bf16[256,2,24,128]{3,0,2,1:T(8,128)(2,1)} async-done(((bf16[64,2,24,128]{3,0,2,1:T(8,128)(2,1)}), bf16[256,2,24,128]{3,0,2,1:T(8,128)(2,1)}) %all-gather.6.cloned.1.call-update) | async-done | bytes 3145744 | tf_op jit(solution)/shard_map/while/body/eval_jaxpr/all_gather | solution.py:119
  (684 shorter events, 813.7 us)
Async XLA Ops:
  6.5 17.2 %copy-start = (bf16[1,512,2304]{2,1,0:T(8,128)(2,1)S(1)}, bf16[1,512,2304]{2,1,0:T(8,128)(2,1)}, u32[]{:S(2)}) copy-start(bf16[1,512,2304]{2,1,0:T(8,128)(2,1)} %param.17) | copy-start | bytes 7077892
  6.5 131.3 %all-gather.4.cloned.1.call-start = ((), (), s32[]{:S(2)}) async-start(), calls=%async_computation.1 | async-start | bytes 1474560 | tf_op jit(solution)/shard_map/all_gather | solution.py:119
  22.8 16.3 %copy-start.6 = (bf16[1,12,2,3072]{3,2,1,0:T(2,128)(2,1)S(1)}, bf16[1,12,2,3072]{3,2,1,0:T(2,128)(2,1)}, u32[]{:S(2)}) copy-start(bf16[1,12,2,3072]{3,2,1,0:T(2,128)(2,1)} %param.22) | copy-start | bytes 442372
  178.7 103.4 %all-gather.6.cloned.1.call-start = ((), (), s32[]{:S(2)}) async-start(), calls=%async_computation.2 | async-start | bytes 3932160 | tf_op jit(solution)/shard_map/while/body/eval_jaxpr/all_gather | solution.py:119
  219.0 119.3 %reduce-scatter.2.cloned.1.call-start = ((), (), s32[]{:S(2)}) async-start(), calls=%async_computation.3 | async-start | bytes 1179648 | tf_op jit(solution)/shard_map/while/body/eval_jaxpr/reduce_scatter | solution.py:181
  340.2 12.8 collective-permute-start
  353.0 102.7 %all-gather.6.cloned.1.call-start = ((), (), s32[]{:S(2)}) async-start(), calls=%async_computation.2 | async-start | bytes 3932160 | tf_op jit(solution)/shard_map/while/body/eval_jaxpr/all_gather | solution.py:119
  393.3 118.7 %reduce-scatter.2.cloned.1.call-start = ((), (), s32[]{:S(2)}) async-start(), calls=%async_computation.3 | async-start | bytes 1179648 | tf_op jit(solution)/shard_map/while/body/eval_jaxpr/reduce_scatter | solution.py:181
  513.8 12.8 collective-permute-start
  526.6 102.7 %all-gather.6.cloned.1.call-start = ((), (), s32[]{:S(2)}) async-start(), calls=%async_computation.2 | async-start | bytes 3932160 | tf_op jit(solution)/shard_map/while/body/eval_jaxpr/all_gather | solution.py:119
  566.9 118.7 %reduce-scatter.2.cloned.1.call-start = ((), (), s32[]{:S(2)}) async-start(), calls=%async_computation.3 | async-start | bytes 1179648 | tf_op jit(solution)/shard_map/while/body/eval_jaxpr/reduce_scatter | solution.py:181
  687.5 12.8 collective-permute-start
  700.3 103.6 %all-gather.6.cloned.1.call-start = ((), (), s32[]{:S(2)}) async-start(), calls=%async_computation.2 | async-start | bytes 3932160 | tf_op jit(solution)/shard_map/while/body/eval_jaxpr/all_gather | solution.py:119
  740.5 120.5 %reduce-scatter.2.cloned.1.call-start = ((), (), s32[]{:S(2)}) async-start(), calls=%async_computation.3 | async-start | bytes 1179648 | tf_op jit(solution)/shard_map/while/body/eval_jaxpr/reduce_scatter | solution.py:181
  863.0 12.8 collective-permute-start
  875.7 102.8 %all-gather.6.cloned.1.call-start = ((), (), s32[]{:S(2)}) async-start(), calls=%async_computation.2 | async-start | bytes 3932160 | tf_op jit(solution)/shard_map/while/body/eval_jaxpr/all_gather | solution.py:119
  916.0 119.9 %reduce-scatter.2.cloned.1.call-start = ((), (), s32[]{:S(2)}) async-start(), calls=%async_computation.3 | async-start | bytes 1179648 | tf_op jit(solution)/shard_map/while/body/eval_jaxpr/reduce_scatter | solution.py:181
  1037.8 12.8 collective-permute-start
  1050.6 102.7 %all-gather.6.cloned.1.call-start = ((), (), s32[]{:S(2)}) async-start(), calls=%async_computation.2 | async-start | bytes 3932160 | tf_op jit(solution)/shard_map/while/body/eval_jaxpr/all_gather | solution.py:119
  1090.9 119.7 %reduce-scatter.2.cloned.1.call-start = ((), (), s32[]{:S(2)}) async-start(), calls=%async_computation.3 | async-start | bytes 1179648 | tf_op jit(solution)/shard_map/while/body/eval_jaxpr/reduce_scatter | solution.py:181
  1212.5 12.8 collective-permute-start
  1225.2 102.7 %all-gather.6.cloned.1.call-start = ((), (), s32[]{:S(2)}) async-start(), calls=%async_computation.2 | async-start | bytes 3932160 | tf_op jit(solution)/shard_map/while/body/eval_jaxpr/all_gather | solution.py:119
  1265.5 119.8 %reduce-scatter.2.cloned.1.call-start = ((), (), s32[]{:S(2)}) async-start(), calls=%async_computation.3 | async-start | bytes 1179648 | tf_op jit(solution)/shard_map/while/body/eval_jaxpr/reduce_scatter | solution.py:181
  1387.2 12.8 collective-permute-start
  (66 other events, 291.6 us)
Sparse Core Ops, SparseCore 0:
  106.7 31.0 all-gather.3
  219.1 62.9 all-gather.5
  320.5 7.1 reduce-scatter.1
  393.4 62.2 all-gather.5
  494.1 7.1 reduce-scatter.1
  567.0 62.2 all-gather.5
  667.8 7.3 reduce-scatter.1
  740.7 63.1 all-gather.5
  843.3 7.1 reduce-scatter.1
  916.2 62.3 all-gather.5
  1018.1 7.1 reduce-scatter.1
  1091.0 62.2 all-gather.5
  1192.8 7.1 reduce-scatter.1
  1265.6 62.2 all-gather.5
  1367.5 7.1 reduce-scatter.1
where the time goes:
time: 1420 us; the launch traced here: 1410 us
  local copies, waits for them, and re-layouts  513 us (36%)
  waiting for transfers between devices  375 us (26%)
  matrix products  302 us (21%)
  other arithmetic  160 us (11%)
  blocking collectives  33 us (2%)
    all_gather x8, waiting for transfers between devices, spread_rows(): return lax.all_gather(key_value, 'row', axis=0, tiled=True)  303 us
    while x140, local copies, waits for them, and re-layouts  242 us
    dot_general x8, matrix products, project(): jnp.dot(piece_rows.reshape(-1, model_width), weights_qkv, preferred_eleme...  138 us
    ppermute x7, waiting for transfers between devices, passed_along(): return lax.ppermute(value, axis, pairs)  72.2 us
    unnamed x16, local copies, waits for them, and re-layouts  61.9 us
    dot_general x7, matrix products, relay_turn(): jnp.einsum('qrhd,krhd->rhqk', queries, cache_table[..., :HD], preferred_e...  61.7 us
    dot_general x7, matrix products, relay_turn(): jnp.einsum('rhqk,krhd->qrhd', weights.astype(jnp.bfloat16), cache_table[....  58.8 us
    dot_general x7, matrix products, relay_turn(): jnp.dot(flat_rows, weights_out, preferred_element_type=jnp.float32)  41.9 us
  transfers between devices with their start and end apart: 22, of which 15 were waited for; matrix products, arithmetic and copies ran while one was open for 21% of the time, Pallas kernels for 0%

commit v1 on v0

--- a/solution.py
+++ b/solution.py
@@ -1,6 +1,8 @@
 import jax
 import jax.numpy as jnp
 from jax import lax
+from jax.experimental import pallas as pl
+from jax.experimental.pallas import tpu as pltpu
 from jax.sharding import PartitionSpec as P
 
 HD = 64
@@ -209,9 +211,258 @@
     return final_state[1][None]
 
 
+HEAD_PAIR = 6 * HD
+DEAD = -1e30
+
+
+def block_body(patch_ref, cell_ref, x_ref, w_ref, gain_ref, cos_ref, sin_ref, bias_ref, old_ref,
+               kv_ref, out_ref):
+    cols, rows, reqs, toks, width = x_ref.shape
+    total_rows = cols * rows * reqs * toks
+    patch = patch_ref[0]
+    x = x_ref[...].reshape(total_rows, width)
+    mixed = jnp.dot(x, w_ref[0], preferred_element_type=jnp.float32)
+    lane = lax.broadcasted_iota(jnp.int32, (total_rows, 2 * HD), 1)
+    low = lane < HD
+    even = lane % 2 == 0
+    cosine = cos_ref[0]
+    sine = sin_ref[0]
+
+    def halves_mean(value):
+        low_sum = jnp.sum(jnp.where(low, value, 0.0), axis=-1, keepdims=True)
+        high_sum = jnp.sum(jnp.where(low, 0.0, value), axis=-1, keepdims=True)
+        return jnp.where(low, low_sum, high_sum) * (1.0 / HD)
+
+    def turned(value, gain):
+        centered = value - halves_mean(value)
+        scaled = centered * lax.rsqrt(halves_mean(centered * centered) + 1e-06) * gain
+        swapped = jnp.where(even, pltpu.roll(scaled, 2 * HD - 1, 1), pltpu.roll(scaled, 1, 1))
+        return scaled * cosine + swapped * sine
+
+    raw = [mixed[:, i * 2 * HD:(i + 1) * 2 * HD] for i in range(3)]
+    done = [turned(raw[i], gain_ref[i:i + 1, :]) for i in range(3)]
+    first_kv = jnp.where(low, pltpu.roll(done[0], HD, 1), pltpu.roll(raw[1], HD, 1))
+    second_kv = jnp.where(low, done[2], raw[2])
+    first_q = jnp.where(low, done[0] * HD ** (-0.5), 0.0)
+    second_q = jnp.where(low, pltpu.roll(done[1], HD, 1) * HD ** (-0.5), 0.0)
+    pairs = [first_kv.astype(jnp.bfloat16), second_kv.astype(jnp.bfloat16)]
+    queries = [first_q.astype(jnp.bfloat16), second_q.astype(jnp.bfloat16)]
+
+    kv_ref[...] = old_ref[...]
+
+    def block_of(c, w, r):
+        start = ((c * rows + w) * reqs + r) * toks
+        return slice(start, start + toks)
+
+    def plen_of(c, w):
+        start = (w * cols + c) * toks
+        return slice(start, start + toks)
+
+    for head in range(2):
+        for c in range(cols):
+            for w in range(rows):
+                for r in range(reqs):
+                    kv_ref[r, head, patch, plen_of(c, w), :] = pairs[head][block_of(c, w, r), :]
+    plen = rows * cols * toks
+    low_out = lax.broadcasted_iota(jnp.int32, (plen, 2 * HD), 1) < HD
+    for r in range(reqs):
+        attended = []
+        for head in range(2):
+            query = jnp.concatenate(
+                [queries[head][block_of(c, w, r), :] for w in range(rows) for c in range(cols)],
+                axis=0,
+            )
+            table = kv_ref[r, head].reshape(-1, 2 * HD)
+            scores = lax.dot_general(
+                query, table, (((1,), (1,)), ((), ())), preferred_element_type=jnp.float32
+            )
+            weights = jnp.exp(scores + bias_ref[r:r + 1, :])
+            totals = jnp.sum(weights, axis=-1, keepdims=True)
+            summed = jnp.dot(
+                weights.astype(jnp.bfloat16), table, preferred_element_type=jnp.float32
+            )
+            attended.append(summed / totals)
+        both = jnp.where(low_out, pltpu.roll(attended[0], HD, 1), attended[1])
+        both = both.astype(jnp.bfloat16)
+        for w in range(rows):
+            for c in range(cols):
+                out_ref[w, c, r] = both[plen_of(c, w), :]
+
+
+def block_call(patch, cell, x, weights, gains, cosine, sine, bias, cache):
+    cols, rows, reqs, toks, width = x.shape
+    pair_count = cache.shape[1] // 2
+    patches, plen = cache.shape[2], cache.shape[3]
+    total_rows = cols * rows * reqs * toks
+    flops = 2 * total_rows * width * HEAD_PAIR * pair_count
+    flops += 8 * total_rows * patches * plen * HD * pair_count * 2
+    grid_spec = pltpu.PrefetchScalarGridSpec(
+        num_scalar_prefetch=2,
+        grid=(pair_count,),
+        in_specs=[
+            pl.BlockSpec(x.shape, lambda j, p, m: (0, 0, 0, 0, 0)),
+            pl.BlockSpec((1, width, HEAD_PAIR), lambda j, p, m: (0, 0, m[0] * pair_count + j)),
+            pl.BlockSpec(gains.shape, lambda j, p, m: (0, 0)),
+            pl.BlockSpec((1, total_rows, 2 * HD), lambda j, p, m: (p[0], 0, 0)),
+            pl.BlockSpec((1, total_rows, 2 * HD), lambda j, p, m: (p[0], 0, 0)),
+            pl.BlockSpec(bias.shape, lambda j, p, m: (0, 0)),
+            pl.BlockSpec((reqs, 2, patches, plen, 2 * HD), lambda j, p, m: (0, j, 0, 0, 0)),
+        ],
+        out_specs=[
+            pl.BlockSpec((reqs, 2, patches, plen, 2 * HD), lambda j, p, m: (0, j, 0, 0, 0)),
+            pl.BlockSpec((rows, cols, reqs, toks, 2 * HD), lambda j, p, m: (0, 0, 0, 0, j)),
+        ],
+    )
+    return pl.pallas_call(
+        block_body,
+        grid_spec=grid_spec,
+        out_shape=[
+            jax.ShapeDtypeStruct(cache.shape, jnp.bfloat16),
+            jax.ShapeDtypeStruct((rows, cols, reqs, toks, pair_count * 2 * HD), jnp.bfloat16),
+        ],
+        compiler_params=pltpu.CompilerParams(vmem_limit_bytes=44 * 1024 * 1024),
+        cost_estimate=pl.CostEstimate(
+            flops=flops, bytes_accessed=20 * 1024 * 1024,
+            transcendentals=2 * pair_count * total_rows * patches * plen,
+        ),
+    )(patch, cell, x, weights, gains, cosine, sine, bias, cache)
+
+
+def modulate_split(values, positions, modulation):
+    is_text = (positions < TXT)[..., None]
+    shifts = jnp.where(is_text, modulation[3], modulation[0])
+    scales = jnp.where(is_text, modulation[4], modulation[1])
+    normed = layer_norm(values.astype(jnp.float32), 1e-05)
+    return (normed * (1.0 + scales) + shifts).astype(jnp.bfloat16)
+
+
+def gather_cells(value):
+    return lax.all_gather(lax.all_gather(value, "row", axis=0), "col", axis=0)
+
+
+def local_split(
+    hidden,
+    patch_counts,
+    timestep,
+    time_table,
+    ada_weight,
+    qkv_weight,
+    out_weight,
+    qk_gain,
+    stale_kv,
+    stale_inputs,
+    recompute_slots,
+):
+    cols = lax.axis_size("col")
+    rows = lax.axis_size("row")
+    section_count = lax.axis_size("section")
+    section = lax.axis_index("section")
+    row = lax.axis_index("row")
+    col = lax.axis_index("col")
+    num_patches, toks, reqs, width = hidden.shape
+    seq = PLEN * num_patches
+    heads_here = stale_kv.shape[3] // rows
+    starts = jnp.cumsum(patch_counts, axis=1) - patch_counts
+    slots = jnp.arange(seq, dtype=jnp.int32)
+    positions = starts[:, slots // PLEN] + slots[None, :] % PLEN
+    live = slots[None, :] % PLEN < patch_counts[:, slots // PLEN]
+    bias = jnp.where(live, 0.0, DEAD).astype(jnp.float32)
+
+    embedding = jax.nn.silu(time_table[timestep[0]]).astype(jnp.bfloat16)
+    mod_part = jnp.dot(embedding, ada_weight[0], preferred_element_type=jnp.float32)
+    modulation = lax.all_gather(mod_part, ("row", "col"), axis=0, tiled=True).reshape(6, width)
+
+    cell_positions = positions.reshape(reqs, num_patches, rows, cols, toks)
+    cell_positions = cell_positions.transpose(1, 3, 2, 0, 4).reshape(num_patches, -1)
+    cosine, sine = rotary_tables(cell_positions)
+    signs = jnp.where(jnp.arange(HD) % 2 == 0, -1.0, 1.0)
+    sine = sine * signs
+    cosine = jnp.concatenate([cosine, cosine], axis=-1)
+    sine = jnp.concatenate([sine, sine], axis=-1)
+    gain_q, gain_k = qk_gain[0, 0], qk_gain[0, 1]
+    ones = jnp.ones_like(gain_q)
+    gains = jnp.stack([
+        jnp.concatenate([gain_q, gain_k]),
+        jnp.concatenate([ones, gain_q]),
+        jnp.concatenate([gain_k, ones]),
+    ])
+
+    rec = recompute_slots.shape[1]
+    rec_toks = rec // (rows * cols)
+    rec_positions = jnp.take_along_axis(positions, recompute_slots, axis=1)
+    my_rec = lax.dynamic_slice_in_dim(rec_positions, (row * cols + col) * rec_toks, rec_toks, 1)
+    rec_normed = modulate_split(stale_inputs[0], my_rec.T, modulation)
+    rec_all = gather_cells(rec_normed)
+
+    def by_cell(table):
+        table = table.reshape(reqs, rows, cols, rec_toks).transpose(2, 1, 3, 0)
+        return table.reshape(-1, reqs)
+
+    rec_places = by_cell(rec_positions)
+    rec_slots = by_cell(recompute_slots)
+    per_row = heads_here * 3 * HD
+    weights_here = lax.dynamic_slice_in_dim(qkv_weight[0], row * per_row, per_row, 1)
+    rec_mixed = jnp.dot(
+        rec_all.reshape(-1, width), weights_here, preferred_element_type=jnp.float32
+    ).reshape(rec, reqs, heads_here, 3, HD)
+    rec_pairs = heads_from(rec_mixed, rec_places, qk_gain[0])[..., HD:]
+    stale_here = lax.dynamic_slice_in_dim(stale_kv[0], row * heads_here, heads_here, 2)
+    stale_here = stale_here.transpose(1, 2, 0, 3)
+    match = (slots[None, :, None] == rec_slots.T[:, None, :])
+    placed = jnp.einsum(
+        "rsi,irhd->rhsd", match.astype(jnp.bfloat16), rec_pairs,
+        preferred_element_type=jnp.float32,
+    ).astype(jnp.bfloat16)
+    replaced = jnp.any(match, axis=-1)[:, None, :, None]
+    cache = jnp.where(replaced, placed, stale_here)
+    cache = cache.reshape(reqs, heads_here, num_patches, PLEN, 2 * HD)
+
+    entering = hidden.transpose(0, 2, 1, 3)
+    out_rows = out_weight[0].reshape(rows, heads_here * HD, width)
+    my_offsets = (row * cols + col) * toks + jnp.arange(toks, dtype=jnp.int32)
+    cell = jnp.reshape(row, (1,)).astype(jnp.int32)
+    leavings = []
+    incoming = entering[0]
+    for turn in range(num_patches + section_count - 1):
+        patch = jnp.clip(turn - section, 0, num_patches - 1).astype(jnp.int32)
+        my_positions = starts[:, patch][:, None] + my_offsets[None, :]
+        if turn == 0 or turn >= num_patches:
+            inputs = incoming
+        else:
+            inputs = jnp.where(section == 0, entering[turn], incoming)
+        normed = modulate_split(inputs, my_positions, modulation)
+        cache, attended = block_call(
+            patch.reshape(1), cell, gather_cells(normed), qkv_weight, gains, cosine, sine, bias,
+            cache,
+        )
+        returned = lax.all_to_all(attended, "row", 0, 0, tiled=True)
+        returned = returned.transpose(1, 2, 3, 0, 4).reshape(cols * reqs * toks, -1)
+        partial = jnp.dot(
+            returned, out_weight[0], preferred_element_type=jnp.float32
+        ).astype(jnp.bfloat16).reshape(cols, reqs, toks, width)
+        mine = lax.dynamic_index_in_dim(partial, col, 0, False)
+        other = lax.dynamic_index_in_dim(partial, 1 - col, 0, False)
+        other = lax.ppermute(other, "col", [(0, 1), (1, 0)])
+        projected = mine.astype(jnp.float32) + other.astype(jnp.float32)
+        is_text = (my_positions < TXT)[..., None]
+        gate_rows = jnp.where(is_text, modulation[5], modulation[2])
+        leaving = (inputs.astype(jnp.float32) + gate_rows * projected).astype(jnp.bfloat16)
+        leavings.append(leaving)
+        if turn < num_patches + section_count - 2:
+            incoming = passed_along(leaving, "section", 1)
+    stacked = jnp.stack(leavings)
+    mine = lax.dynamic_slice_in_dim(stacked, section, num_patches, 0)
+    return mine.transpose(0, 2, 1, 3)[None]
+
+
+def fits_split(mesh):
+    heads = 48 // mesh.shape["col"]
+    return mesh.shape["col"] == 2 and heads % (2 * mesh.shape["row"]) == 0
+
+
 def solution(mesh):
     return jax.shard_map(
-        local,
+        local_split if fits_split(mesh) else local,
         mesh=mesh,
         in_specs=(
             P(None, ("row", "col"), None, None),

time: 1420 us -> 811 us (0.57)
  local copies, waits for them, and re-layouts: 513 us -> 76.7 us
  matrix products: 302 us -> 22.2 us
  other arithmetic: 160 us -> 34.7 us
  Pallas kernels: 0 us -> 117 us
  blocking collectives: 33 us -> 139 us
    dot_general x30 -> x10, matrix products: 302 us -> 22.2 us  [the longest x7 13.6 us: local_split(): jnp.dot(returned, out_weight[0], preferred_element_type=jnp.float32)]
    while x140 -> x0, local copies, waits for them, and re-layouts: 242 us -> none
    pallas_call x0 -> x7, Pallas kernels: none -> 117 us  [block_call(): pl.pallas_call(block_body, grid_spec=grid_spec, out_shape=[jax.ShapeDtype...]
    all_to_all x0 -> x6, blocking collectives: none -> 99.9 us  [local_split(): returned = lax.all_to_all(attended, 'row', 0, 0, tiled=True)]
    reshape x30 -> x6, local copies, waits for them, and re-layouts: 48.5 us -> 1.21 us  [the longest x3 1.03 us: rotary_tables(): phase_parts.append(jnp.repeat(phase_part, 2, axis=-1))]
    select_n x17 -> x5, other arithmetic: 42.9 us -> 0.04 us  [the longest x3 0.03 us: local_split(): positions = starts[:, slots // PLEN] + slots[None, :] % PLEN]
    unnamed x16 -> x113, local copies, waits for them, and re-layouts: 61.9 us -> 22 us
    dynamic_update_slice x14 -> x0, local copies, waits for them, and re-layouts: 37 us -> none  [the longest x7 28.9 us: relay_turn(): cache_table = lax.dynamic_update_slice(cache_table, new_block, block_start)]
  transfers between devices with their start and end apart: 22 -> 29, of which waited for: 15 -> 26; matrix products, arithmetic and copies ran while one was open for 21% -> 8% of each run, Pallas kernels for 0% -> 0%
where the time goes in v1:
time: 811 us; the launch traced here: 805 us
  waiting for transfers between devices  388 us (48%)
  blocking collectives  139 us (17%)
  Pallas kernels  117 us (14%)
  local copies, waits for them, and re-layouts  76.7 us (9%)
  other arithmetic  34.7 us (4%)
  matrix products  22.2 us (3%)
  between operations  15.4 us (2%)
  starting transfers between devices  12.3 us (2%)
    all_gather x15, waiting for transfers between devices, gather_cells(): return lax.all_gather(lax.all_gather(value, 'row', axis=0), 'col', axis=0)  294 us
    pallas_call x7, Pallas kernels, block_call(): pl.pallas_call(block_body, grid_spec=grid_spec, out_shape=[jax.ShapeDtype...  117 us
    all_to_all x6, blocking collectives, local_split(): returned = lax.all_to_all(attended, 'row', 0, 0, tiled=True)  99.9 us
    ppermute x6, waiting for transfers between devices, passed_along(): return lax.ppermute(value, axis, pairs)  70.7 us
    all_gather x1, blocking collectives, gather_cells(): return lax.all_gather(lax.all_gather(value, 'row', axis=0), 'col', axis=0)  24.4 us
    unnamed x113, local copies, waits for them, and re-layouts  22 us
    dot_general x2, local copies, waits for them, and re-layouts, local_split(): jnp.dot(rec_all.reshape(-1, width), weights_here, preferred_element_type=...  16.9 us
  transfers between devices with their start and end apart: 29, of which 26 were waited for; matrix products, arithmetic and copies ran while one was open for 8% of the time, Pallas kernels for 0%

profile of v1, /device:TPU:6, one launch (start us, length us, event | category | flops | bytes accessed | tf_op | source)
XLA Modules:
  0.0 805.0 jit_solution(1198887665975038273)
XLA Ops:
  9.3 14.3 %all-gather.14 = f32[8,1,2304]{2,1,0:T(1,128)S(1)} all-gather(f32[1,1,2304]{2,1,0:T(1,128)S(1)} %convolution_bitcast_fusion), channel_id=1, replica_groups=mesh['section'=4,'row'=4,'col'=2] {'row','col'}, dimensions={0}, use_global_device_ids=true | all-gather | bytes 82944 | tf_op jit(solution)/shard_map/all_gather | solution.py:373
  33.3 24.4 %all_gather.99 = bf16[4,12,2,3072]{3,2,1,0:T(2,128)(2,1)} all-gather(bf16[1,12,2,3072]{3,2,1,0:T(2,128)(2,1)S(1)} %fusion.114), channel_id=1, replica_groups=mesh['section'=4,'row'=4,'col'=2] {'row'}, dimensions={0}, use_global_device_ids=true | all-gather | bytes 737280 | tf_op jit(solution)/shard_map/all_gather | solution.py:340
  121.2 17.1 %shard_map.109 = (bf16[2,6,4,256,128]{4,3,2,1,0:T(8,128)(2,1)S(1)}, bf16[4,2,2,32,384]{4,3,2,1,0:T(8,128)(2,1)}) custom-call(s32[1]{0:T(128)} %bitcast.6.patch_ref, s32[1]{0:T(128)} %bitcast.7.cell_ref, bf16[2,4,2,32,3072]{4,3,2,1,0:T(8,128)(2,1)S(1)} %bitcast.327, bf16[1,3072,4608]{2,1,0:T(8,128)(2,1)} %w_ref.13, f32[3,128]{1,0:T(4,128)S(1)} %pad_maximum_fusion.5.gain_ref, ...), custom_call_target="tpu_custom_call" | custom-call | flops 5234491392 | bytes 20971520 | tf_op jit(solution)/shard_map/pallas_call | solution.py:316
  181.9 36.2 %all-gather.37.cloned.1.call-done = bf16[8,32,3072]{2,1,0:T(8,128)(2,1)} async-done(((bf16[2,32,3072]{2,1,0:T(8,128)(2,1)}), bf16[8,32,3072]{2,1,0:T(8,128)(2,1)}) %all-gather.37.cloned.1.call-update) | async-done | bytes 1572880 | tf_op jit(solution)/shard_map/all_gather | solution.py:340
  232.7 16.4 %shard_map.110 = (bf16[2,6,4,256,128]{4,3,2,1,0:T(8,128)(2,1)S(1)}, bf16[4,2,2,32,384]{4,3,2,1,0:T(8,128)(2,1)S(1)}) custom-call(s32[1]{0:T(128)} %bitcast.65.patch_ref, s32[1]{0:T(128)} %bitcast.7.cell_ref, bf16[2,4,2,32,3072]{4,3,2,1,0:T(8,128)(2,1)S(1)} %bitcast.329, bf16[1,3072,4608]{2,1,0:T(8,128)(2,1)} %w_ref.13, ...), custom_call_target="tpu_custom_call" | custom-call | flops 5234491392 | bytes 20971520 | tf_op jit(solution)/shard_map/pallas_call | solution.py:316
  249.1 17.0 %all_to_all.35 = bf16[4,2,2,32,384]{4,3,2,1,0:T(8,128)(2,1)S(1)} all-to-all(bf16[4,2,2,32,384]{4,3,2,1,0:T(8,128)(2,1)S(1)} %get-tuple-element.20), channel_id=1, replica_groups=mesh['section'=4,'row'=4,'col'=2] {'row'}, dimensions={0} | all-to-all | bytes 786432 | tf_op jit(solution)/shard_map/all_to_all | solution.py:438
  286.9 36.2 %all-gather.41.cloned.1.call-done = bf16[8,32,3072]{2,1,0:T(8,128)(2,1)} async-done(((bf16[2,32,3072]{2,1,0:T(8,128)(2,1)}), bf16[8,32,3072]{2,1,0:T(8,128)(2,1)}) %all-gather.41.cloned.1.call-update) | async-done | bytes 1572880 | tf_op jit(solution)/shard_map/all_gather | solution.py:340
  323.2 12.8 %all-gather.43.cloned.1.call-done = bf16[8,2,32,3072]{3,2,1,0:T(8,128)(2,1)} async-done(((bf16[4,2,32,3072]{3,2,1,0:T(8,128)(2,1)}), bf16[8,2,32,3072]{3,2,1,0:T(8,128)(2,1)}) %all-gather.43.cloned.1.call-update) | async-done | bytes 3145744 | tf_op jit(solution)/shard_map/all_gather | solution.py:340
  337.8 16.4 %shard_map.111 = (bf16[2,6,4,256,128]{4,3,2,1,0:T(8,128)(2,1)S(1)}, bf16[4,2,2,32,384]{4,3,2,1,0:T(8,128)(2,1)S(1)}) custom-call(s32[1]{0:T(128)} %bitcast.75.patch_ref, s32[1]{0:T(128)} %bitcast.7.cell_ref, bf16[2,4,2,32,3072]{4,3,2,1,0:T(8,128)(2,1)S(1)} %bitcast.330, bf16[1,3072,4608]{2,1,0:T(8,128)(2,1)} %w_ref.13, ...), custom_call_target="tpu_custom_call" | custom-call | flops 5234491392 | bytes 20971520 | tf_op jit(solution)/shard_map/pallas_call | solution.py:316
  354.2 16.5 %all_to_all.36 = bf16[4,2,2,32,384]{4,3,2,1,0:T(8,128)(2,1)S(1)} all-to-all(bf16[4,2,2,32,384]{4,3,2,1,0:T(8,128)(2,1)S(1)} %get-tuple-element.22), channel_id=1, replica_groups=mesh['section'=4,'row'=4,'col'=2] {'row'}, dimensions={0} | all-to-all | bytes 786432 | tf_op jit(solution)/shard_map/all_to_all | solution.py:438
  391.6 36.2 %all-gather.45.cloned.1.call-done = bf16[8,32,3072]{2,1,0:T(8,128)(2,1)} async-done(((bf16[2,32,3072]{2,1,0:T(8,128)(2,1)}), bf16[8,32,3072]{2,1,0:T(8,128)(2,1)}) %all-gather.45.cloned.1.call-update) | async-done | bytes 1572880 | tf_op jit(solution)/shard_map/all_gather | solution.py:340
  428.0 12.8 %all-gather.47.cloned.1.call-done = bf16[8,2,32,3072]{3,2,1,0:T(8,128)(2,1)} async-done(((bf16[4,2,32,3072]{3,2,1,0:T(8,128)(2,1)}), bf16[8,2,32,3072]{3,2,1,0:T(8,128)(2,1)}) %all-gather.47.cloned.1.call-update) | async-done | bytes 3145744 | tf_op jit(solution)/shard_map/all_gather | solution.py:340
  442.6 16.6 %shard_map.112 = (bf16[2,6,4,256,128]{4,3,2,1,0:T(8,128)(2,1)S(1)}, bf16[4,2,2,32,384]{4,3,2,1,0:T(8,128)(2,1)S(1)}) custom-call(s32[1]{0:T(128)} %bitcast.85.patch_ref, s32[1]{0:T(128)} %bitcast.7.cell_ref, bf16[2,4,2,32,3072]{4,3,2,1,0:T(8,128)(2,1)S(1)} %bitcast.331, bf16[1,3072,4608]{2,1,0:T(8,128)(2,1)} %w_ref.13, ...), custom_call_target="tpu_custom_call" | custom-call | flops 5234491392 | bytes 20971520 | tf_op jit(solution)/shard_map/pallas_call | solution.py:316
  459.2 16.5 %all_to_all.37 = bf16[4,2,2,32,384]{4,3,2,1,0:T(8,128)(2,1)S(1)} all-to-all(bf16[4,2,2,32,384]{4,3,2,1,0:T(8,128)(2,1)S(1)} %get-tuple-element.24), channel_id=1, replica_groups=mesh['section'=4,'row'=4,'col'=2] {'row'}, dimensions={0} | all-to-all | bytes 786432 | tf_op jit(solution)/shard_map/all_to_all | solution.py:438
  495.3 36.2 %all-gather.49.cloned.1.call-done = bf16[8,32,3072]{2,1,0:T(8,128)(2,1)} async-done(((bf16[2,32,3072]{2,1,0:T(8,128)(2,1)}), bf16[8,32,3072]{2,1,0:T(8,128)(2,1)}) %all-gather.49.cloned.1.call-update) | async-done | bytes 1572880 | tf_op jit(solution)/shard_map/all_gather | solution.py:340
  531.6 12.8 %all-gather.51.cloned.1.call-done = bf16[8,2,32,3072]{3,2,1,0:T(8,128)(2,1)} async-done(((bf16[4,2,32,3072]{3,2,1,0:T(8,128)(2,1)}), bf16[8,2,32,3072]{3,2,1,0:T(8,128)(2,1)}) %all-gather.51.cloned.1.call-update) | async-done | bytes 3145744 | tf_op jit(solution)/shard_map/all_gather | solution.py:340
  546.3 16.4 %shard_map.113 = (bf16[2,6,4,256,128]{4,3,2,1,0:T(8,128)(2,1)S(1)}, bf16[4,2,2,32,384]{4,3,2,1,0:T(8,128)(2,1)S(1)}) custom-call(s32[1]{0:T(128)} %bitcast.94.patch_ref, s32[1]{0:T(128)} %bitcast.7.cell_ref, bf16[2,4,2,32,3072]{4,3,2,1,0:T(8,128)(2,1)S(1)} %bitcast.332, bf16[1,3072,4608]{2,1,0:T(8,128)(2,1)} %w_ref.13, ...), custom_call_target="tpu_custom_call" | custom-call | flops 5234491392 | bytes 20971520 | tf_op jit(solution)/shard_map/pallas_call | solution.py:316
  562.7 16.8 %all_to_all.38 = bf16[4,2,2,32,384]{4,3,2,1,0:T(8,128)(2,1)S(1)} all-to-all(bf16[4,2,2,32,384]{4,3,2,1,0:T(8,128)(2,1)S(1)} %get-tuple-element.26), channel_id=1, replica_groups=mesh['section'=4,'row'=4,'col'=2] {'row'}, dimensions={0} | all-to-all | bytes 786432 | tf_op jit(solution)/shard_map/all_to_all | solution.py:438
  599.0 36.2 %all-gather.53.cloned.1.call-done = bf16[8,32,3072]{2,1,0:T(8,128)(2,1)} async-done(((bf16[2,32,3072]{2,1,0:T(8,128)(2,1)}), bf16[8,32,3072]{2,1,0:T(8,128)(2,1)}) %all-gather.53.cloned.1.call-update) | async-done | bytes 1572880 | tf_op jit(solution)/shard_map/all_gather | solution.py:340
  649.9 16.4 %shard_map.114 = (bf16[2,6,4,256,128]{4,3,2,1,0:T(8,128)(2,1)S(1)}, bf16[4,2,2,32,384]{4,3,2,1,0:T(8,128)(2,1)S(1)}) custom-call(s32[1]{0:T(128)} %bitcast.103.patch_ref, s32[1]{0:T(128)} %bitcast.7.cell_ref, bf16[2,4,2,32,3072]{4,3,2,1,0:T(8,128)(2,1)S(1)} %bitcast.333, bf16[1,3072,4608]{2,1,0:T(8,128)(2,1)} %w_ref.13, ...), custom_call_target="tpu_custom_call" | custom-call | flops 5234491392 | bytes 20971520 | tf_op jit(solution)/shard_map/pallas_call | solution.py:316
  666.4 16.5 %all_to_all.39 = bf16[4,2,2,32,384]{4,3,2,1,0:T(8,128)(2,1)S(1)} all-to-all(bf16[4,2,2,32,384]{4,3,2,1,0:T(8,128)(2,1)S(1)} %get-tuple-element.28), channel_id=1, replica_groups=mesh['section'=4,'row'=4,'col'=2] {'row'}, dimensions={0} | all-to-all | bytes 786432 | tf_op jit(solution)/shard_map/all_to_all | solution.py:438
  702.4 36.2 %all-gather.57.cloned.1.call-done = bf16[8,32,3072]{2,1,0:T(8,128)(2,1)} async-done(((bf16[2,32,3072]{2,1,0:T(8,128)(2,1)}), bf16[8,32,3072]{2,1,0:T(8,128)(2,1)}) %all-gather.57.cloned.1.call-update) | async-done | bytes 1572880 | tf_op jit(solution)/shard_map/all_gather | solution.py:340
  753.2 17.4 %shard_map.115 = (bf16[2,6,4,256,128]{4,3,2,1,0:T(8,128)(2,1)}, bf16[4,2,2,32,384]{4,3,2,1,0:T(8,128)(2,1)S(1)}) custom-call(s32[1]{0:T(128)} %bitcast.112.patch_ref, s32[1]{0:T(128)} %bitcast.7.cell_ref, bf16[2,4,2,32,3072]{4,3,2,1,0:T(8,128)(2,1)S(1)} %bitcast.328, bf16[1,3072,4608]{2,1,0:T(8,128)(2,1)} %w_ref.13, ...), custom_call_target="tpu_custom_call" | custom-call | flops 5234491392 | bytes 20971520 | tf_op jit(solution)/shard_map/pallas_call | solution.py:316
  770.7 16.5 %all_to_all.40 = bf16[4,2,2,32,384]{4,3,2,1,0:T(8,128)(2,1)S(1)} all-to-all(bf16[4,2,2,32,384]{4,3,2,1,0:T(8,128)(2,1)S(1)} %get-tuple-element.30), channel_id=1, replica_groups=mesh['section'=4,'row'=4,'col'=2] {'row'}, dimensions={0} | all-to-all | bytes 786432 | tf_op jit(solution)/shard_map/all_to_all | solution.py:438
  (351 shorter events, 278.7 us)
Async XLA Ops:
  6.5 98.4 %all-gather.31.cloned.1.call-start = ((), (), s32[]{:S(2)}) async-start(), calls=%async_computation.7 | async-start | bytes 1966080 | tf_op jit(solution)/shard_map/all_gather | solution.py:340
  27.1 77.9 %all-gather.35.cloned.1.call-start = ((), (), s32[]{:S(2)}) async-start(), calls=%async_computation.9 | async-start | bytes 1769472 | tf_op jit(solution)/shard_map/all_gather | solution.py:340
  57.7 61.7 %all-gather.33.cloned.1.call-start = ((), (), s32[]{:S(2)}) async-start(), calls=%async_computation.8 | async-start | bytes 4718592 | tf_op jit(solution)/shard_map/all_gather | solution.py:340
  139.9 14.9 %all-to-all-start = ((bf16[4,2,2,32,384]{4,3,2,1,0:T(8,128)(2,1)}), bf16[4,2,2,32,384]{4,3,2,1,0:T(8,128)(2,1)S(1)}, u32[]{:S(2)}, u32[]{:S(2)}) async-start(bf16[4,2,2,32,384]{4,3,2,1,0:T(8,128)(2,1)} %get-tuple-element.18), calls=%async_computation | async-start | bytes 786432 | tf_op jit(solution)/shard_map/all_to_all | solution.py:438
  143.4 74.8 %all-gather.37.cloned.1.call-start = ((), (), s32[]{:S(2)}) async-start(), calls=%async_computation.10 | async-start | bytes 1966080 | tf_op jit(solution)/shard_map/all_gather | solution.py:340
  161.2 2.1 collective-permute-start
  165.6 13.2 %collective-permute-start.1 = (bf16[2,32,3072]{2,1,0:T(8,128)(2,1)}, bf16[2,32,3072]{2,1,0:T(8,128)(2,1)S(1)}, u32[]{:S(2)}, u32[]{:S(2)}) collective-permute-start(bf16[2,32,3072]{2,1,0:T(8,128)(2,1)} %get-tuple-element.48), channel_id=1, source_target_pairs={{0,8},{8,16},{16,24},{1,9},{9,17},{17,25},{2,10},{10,18},{18,26},{... | collective-permute-start | bytes 1179656 | tf_op jit(solution)/shard_map/ppermute | solution.py:18
  181.8 49.0 %all-gather.39.cloned.1.call-start = ((), (), s32[]{:S(2)}) async-start(), calls=%async_computation.11 | async-start | bytes 4718592 | tf_op jit(solution)/shard_map/all_gather | solution.py:340
  218.2 104.9 %all-gather.41.cloned.1.call-start = ((), (), s32[]{:S(2)}) async-start(), calls=%async_computation.12 | async-start | bytes 1966080 | tf_op jit(solution)/shard_map/all_gather | solution.py:340
  267.9 1.8 collective-permute-start.2
  270.7 13.0 %collective-permute-start.3 = (bf16[2,32,3072]{2,1,0:T(8,128)(2,1)S(1)}, bf16[2,32,3072]{2,1,0:T(8,128)(2,1)S(1)}, u32[]{:S(2)}, u32[]{:S(2)}) collective-permute-start(bf16[2,32,3072]{2,1,0:T(8,128)(2,1)S(1)} %get-tuple-element.44), channel_id=1, source_target_pairs={{0,8},{8,16},{16,24},{1,9},{9,17},{17,25},{2,10},{10,18},{18,26},{... | collective-permute-start | bytes 1179656 | tf_op jit(solution)/shard_map/ppermute | solution.py:18
  286.8 49.1 %all-gather.43.cloned.1.call-start = ((), (), s32[]{:S(2)}) async-start(), calls=%async_computation.13 | async-start | bytes 4718592 | tf_op jit(solution)/shard_map/all_gather | solution.py:340
  323.1 104.8 %all-gather.45.cloned.1.call-start = ((), (), s32[]{:S(2)}) async-start(), calls=%async_computation.14 | async-start | bytes 1966080 | tf_op jit(solution)/shard_map/all_gather | solution.py:340
  375.4 13.0 %collective-permute-start.5 = (bf16[2,32,3072]{2,1,0:T(8,128)(2,1)S(1)}, bf16[2,32,3072]{2,1,0:T(8,128)(2,1)S(1)}, u32[]{:S(2)}, u32[]{:S(2)}) collective-permute-start(bf16[2,32,3072]{2,1,0:T(8,128)(2,1)S(1)} %get-tuple-element.40), channel_id=1, source_target_pairs={{0,8},{8,16},{16,24},{1,9},{9,17},{17,25},{2,10},{10,18},{18,26},{... | collective-permute-start | bytes 1179656 | tf_op jit(solution)/shard_map/ppermute | solution.py:18
  391.6 49.1 %all-gather.47.cloned.1.call-start = ((), (), s32[]{:S(2)}) async-start(), calls=%async_computation.15 | async-start | bytes 4718592 | tf_op jit(solution)/shard_map/all_gather | solution.py:340
  427.9 103.6 %all-gather.49.cloned.1.call-start = ((), (), s32[]{:S(2)}) async-start(), calls=%async_computation.16 | async-start | bytes 1966080 | tf_op jit(solution)/shard_map/all_gather | solution.py:340
  480.4 13.0 %collective-permute-start.7 = (bf16[2,32,3072]{2,1,0:T(8,128)(2,1)S(1)}, bf16[2,32,3072]{2,1,0:T(8,128)(2,1)S(1)}, u32[]{:S(2)}, u32[]{:S(2)}) collective-permute-start(bf16[2,32,3072]{2,1,0:T(8,128)(2,1)S(1)} %get-tuple-element.36), channel_id=1, source_target_pairs={{0,8},{8,16},{16,24},{1,9},{9,17},{17,25},{2,10},{10,18},{18,26},{... | collective-permute-start | bytes 1179656 | tf_op jit(solution)/shard_map/ppermute | solution.py:18
  495.2 49.1 %all-gather.51.cloned.1.call-start = ((), (), s32[]{:S(2)}) async-start(), calls=%async_computation.17 | async-start | bytes 4718592 | tf_op jit(solution)/shard_map/all_gather | solution.py:340
  531.6 103.7 %all-gather.53.cloned.1.call-start = ((), (), s32[]{:S(2)}) async-start(), calls=%async_computation.18 | async-start | bytes 1966080 | tf_op jit(solution)/shard_map/all_gather | solution.py:340
  584.1 13.0 %collective-permute-start.9 = (bf16[2,32,3072]{2,1,0:T(8,128)(2,1)S(1)}, bf16[2,32,3072]{2,1,0:T(8,128)(2,1)S(1)}, u32[]{:S(2)}, u32[]{:S(2)}) collective-permute-start(bf16[2,32,3072]{2,1,0:T(8,128)(2,1)S(1)} %get-tuple-element.34), channel_id=1, source_target_pairs={{0,8},{8,16},{16,24},{1,9},{9,17},{17,25},{2,10},{10,18},{18,26},{... | collective-permute-start | bytes 1179656 | tf_op jit(solution)/shard_map/ppermute | solution.py:18
  598.9 49.1 %all-gather.55.cloned.1.call-start = ((), (), s32[]{:S(2)}) async-start(), calls=%async_computation.19 | async-start | bytes 4718592 | tf_op jit(solution)/shard_map/all_gather | solution.py:340
  635.2 103.4 %all-gather.57.cloned.1.call-start = ((), (), s32[]{:S(2)}) async-start(), calls=%async_computation.20 | async-start | bytes 1966080 | tf_op jit(solution)/shard_map/all_gather | solution.py:340
  687.5 13.0 %collective-permute-start.11 = (bf16[2,32,3072]{2,1,0:T(8,128)(2,1)S(1)}, bf16[2,32,3072]{2,1,0:T(8,128)(2,1)S(1)}, u32[]{:S(2)}, u32[]{:S(2)}) collective-permute-start(bf16[2,32,3072]{2,1,0:T(8,128)(2,1)S(1)} %get-tuple-element.32), channel_id=1, source_target_pairs={{0,8},{8,16},{16,24},{1,9},{9,17},{17,25},{2,10},{10,18},{18,26},{... | collective-permute-start | bytes 1179656 | tf_op jit(solution)/shard_map/ppermute | solution.py:18
  702.4 49.0 %all-gather.59.cloned.1.call-start = ((), (), s32[]{:S(2)}) async-start(), calls=%async_computation.21 | async-start | bytes 4718592 | tf_op jit(solution)/shard_map/all_gather | solution.py:340
  (57 other events, 1192.6 us)
Sparse Core Ops, SparseCore 0:
  27.2 46.6 all-gather.30
  75.5 8.4 all-gather.34
  105.1 12.4 all-gather.32
  182.0 36.1 all-gather.36
  219.5 11.2 all-gather.38
  286.9 36.1 all-gather.40
  324.6 11.2 all-gather.42
  391.7 36.1 all-gather.44
  429.4 11.2 all-gather.46
  495.4 36.1 all-gather.48
  533.1 11.2 all-gather.50
  599.1 36.1 all-gather.52
  636.8 11.2 all-gather.54
  702.5 36.1 all-gather.56
  740.1 11.2 all-gather.58

commit v2 on v1

--- a/solution.py
+++ b/solution.py
@@ -336,8 +336,177 @@
     return (normed * (1.0 + scales) + shifts).astype(jnp.bfloat16)
 
 
-def gather_cells(value):
-    return lax.all_gather(lax.all_gather(value, "row", axis=0), "col", axis=0)
+def gather_body(x_ref, out_ref, own_sem, line_send, line_recv, side_send, side_recv):
+    chunks = x_ref.shape[0]
+    rows = out_ref.shape[1]
+    w = lax.axis_index("row")
+    c = lax.axis_index("col")
+    sibling = {"col": 1 - c}
+    barrier = pltpu.get_barrier_semaphore()
+    has = {1: w < rows - 1, -1: w > 0}
+
+    def greet(way):
+        @pl.when(has[way])
+        def _():
+            pl.semaphore_signal(barrier, inc=1, device_id={"row": w + way},
+                                device_id_type=pl.DeviceIdType.MESH)
+
+    pl.semaphore_signal(barrier, inc=1, device_id=sibling, device_id_type=pl.DeviceIdType.MESH)
+    greet(1)
+    greet(-1)
+    inside = has[1] & has[-1]
+
+    @pl.when(inside)
+    def _():
+        pl.semaphore_wait(barrier, 3)
+
+    @pl.when(jnp.logical_not(inside))
+    def _():
+        pl.semaphore_wait(barrier, 2)
+
+    def line_copy(way, step, chunk):
+        block = w - way * step
+        source = x_ref.at[chunk] if step == 0 else out_ref.at[c, block, chunk]
+        lane = 0 if way == 1 else 1
+        return pltpu.make_async_remote_copy(
+            src_ref=source, dst_ref=out_ref.at[c, block, chunk],
+            send_sem=line_send.at[lane, step, chunk], recv_sem=line_recv.at[lane, step, chunk],
+            device_id={"row": w + way}, device_id_type=pl.DeviceIdType.MESH,
+        )
+
+    def arrival(way, step, chunk):
+        block = w - way * (step + 1)
+        lane = 0 if way == 1 else 1
+        return pltpu.make_async_remote_copy(
+            src_ref=x_ref.at[chunk], dst_ref=out_ref.at[c, block, chunk],
+            send_sem=line_send.at[lane, step, chunk], recv_sem=line_recv.at[lane, step, chunk],
+            device_id={"row": w + way}, device_id_type=pl.DeviceIdType.MESH,
+        )
+
+    def side_copy(place, block, chunk):
+        source = x_ref.at[chunk] if place == 0 else out_ref.at[c, block, chunk]
+        return pltpu.make_async_remote_copy(
+            src_ref=source, dst_ref=out_ref.at[c, block, chunk],
+            send_sem=side_send.at[place, chunk], recv_sem=side_recv.at[place, chunk],
+            device_id=sibling, device_id_type=pl.DeviceIdType.MESH,
+        )
+
+    def side_arrival(place, block, chunk):
+        return pltpu.make_async_remote_copy(
+            src_ref=x_ref.at[chunk], dst_ref=out_ref.at[1 - c, block, chunk],
+            send_sem=side_send.at[place, chunk], recv_sem=side_recv.at[place, chunk],
+            device_id=sibling, device_id_type=pl.DeviceIdType.MESH,
+        )
+
+    def arrives(way, step):
+        return w >= step + 1 if way == 1 else w <= rows - 2 - step
+
+    def leaves(way, step):
+        held = w >= step if way == 1 else w <= rows - 1 - step
+        return has[way] & held
+
+    def place_of(way, step):
+        return 1 + step if way == 1 else rows + step
+
+    for chunk in range(chunks):
+        for way in (1, -1):
+            @pl.when(leaves(way, 0))
+            def _():
+                line_copy(way, 0, chunk).start()
+    own = []
+    for chunk in range(chunks):
+        side_copy(0, w, chunk).start()
+        kept = pltpu.make_async_copy(x_ref.at[chunk], out_ref.at[c, w, chunk], own_sem.at[chunk])
+        kept.start()
+        own.append(kept)
+    for step in range(rows - 1):
+        for chunk in range(chunks):
+            for way in (1, -1):
+                @pl.when(arrives(way, step))
+                def _():
+                    arrival(way, step, chunk).wait_recv()
+                    if step + 1 < rows - 1:
+                        @pl.when(leaves(way, step + 1))
+                        def _():
+                            line_copy(way, step + 1, chunk).start()
+                    side_copy(place_of(way, step), w - way * (step + 1), chunk).start()
+    for chunk in range(chunks):
+        own[chunk].wait()
+        side_copy(0, w, chunk).wait_send()
+        side_arrival(0, w, chunk).wait_recv()
+        for step in range(rows - 1):
+            for way in (1, -1):
+                @pl.when(leaves(way, step))
+                def _():
+                    line_copy(way, step, chunk).wait_send()
+
+                @pl.when(arrives(way, step))
+                def _():
+                    block = w - way * (step + 1)
+                    side_copy(place_of(way, step), block, chunk).wait_send()
+                    side_arrival(place_of(way, step), block, chunk).wait_recv()
+
+
+def gather_tokens(value, rows, cols, number):
+    chunks = value.shape[0]
+    steps = rows - 1
+    return pl.pallas_call(
+        gather_body,
+        out_shape=jax.ShapeDtypeStruct((cols, rows) + value.shape, value.dtype),
+        in_specs=[pl.BlockSpec(memory_space=pl.ANY)],
+        out_specs=pl.BlockSpec(memory_space=pl.ANY),
+        scratch_shapes=[
+            pltpu.SemaphoreType.DMA((chunks,)),
+            pltpu.SemaphoreType.DMA((2, steps, chunks)),
+            pltpu.SemaphoreType.DMA((2, steps, chunks)),
+            pltpu.SemaphoreType.DMA((2 * steps + 1, chunks)),
+            pltpu.SemaphoreType.DMA((2 * steps + 1, chunks)),
+        ],
+        compiler_params=pltpu.CompilerParams(collective_id=number, has_side_effects=True),
+        cost_estimate=pl.CostEstimate(flops=0, bytes_accessed=40 * 1024 * 1024, transcendentals=0),
+    )(value)
+
+
+def exchange_body(x_ref, out_ref, own_sem, send_sem, recv_sem):
+    rows = x_ref.shape[0]
+    w = lax.axis_index("row")
+    barrier = pltpu.get_barrier_semaphore()
+    for way in range(1, rows):
+        pl.semaphore_signal(barrier, inc=1, device_id={"row": lax.rem(w + way, rows)},
+                            device_id_type=pl.DeviceIdType.MESH)
+    pl.semaphore_wait(barrier, rows - 1)
+    copies = []
+    for way in range(1, rows):
+        target = lax.rem(w + way, rows)
+        copy = pltpu.make_async_remote_copy(
+            src_ref=x_ref.at[target], dst_ref=out_ref.at[w],
+            send_sem=send_sem.at[way - 1], recv_sem=recv_sem.at[way - 1],
+            device_id={"row": target}, device_id_type=pl.DeviceIdType.MESH,
+        )
+        copy.start()
+        copies.append(copy)
+    kept = pltpu.make_async_copy(x_ref.at[w], out_ref.at[w], own_sem)
+    kept.start()
+    for copy in copies:
+        copy.wait()
+    kept.wait()
+
+
+def exchange_rows(value, number):
+    rows = value.shape[0]
+    return pl.pallas_call(
+        exchange_body,
+        out_shape=jax.ShapeDtypeStruct(value.shape, value.dtype),
+        in_specs=[pl.BlockSpec(memory_space=pl.ANY)],
+        out_specs=pl.BlockSpec(memory_space=pl.ANY),
+        scratch_shapes=[
+            pltpu.SemaphoreType.DMA,
+            pltpu.SemaphoreType.DMA((rows - 1,)),
+            pltpu.SemaphoreType.DMA((rows - 1,)),
+        ],
+        compiler_params=pltpu.CompilerParams(collective_id=number, has_side_effects=True),
+        cost_estimate=pl.CostEstimate(flops=0, bytes_accessed=16 * 1024 * 1024, transcendentals=0),
+    )(value)
 
 
 def local_split(
@@ -392,7 +561,18 @@
     rec_positions = jnp.take_along_axis(positions, recompute_slots, axis=1)
     my_rec = lax.dynamic_slice_in_dim(rec_positions, (row * cols + col) * rec_toks, rec_toks, 1)
     rec_normed = modulate_split(stale_inputs[0], my_rec.T, modulation)
-    rec_all = gather_cells(rec_normed)
+    entering = hidden.transpose(0, 2, 1, 3)
+    my_offsets = (row * cols + col) * toks + jnp.arange(toks, dtype=jnp.int32)
+    rec_part = rec_normed.reshape(rec_toks * reqs, width)
+    padded = -(-rec_toks * reqs // toks) * toks
+    rec_part = jnp.pad(rec_part, ((0, padded - rec_toks * reqs), (0, 0)))
+    first_positions = starts[:, 0][:, None] + my_offsets[None, :]
+    first_normed = modulate_split(entering[0], first_positions, modulation)
+    first_all = gather_tokens(
+        jnp.concatenate([first_normed, rec_part.reshape(-1, toks, width)], axis=0), rows, cols, 0
+    )
+    rec_all = first_all[:, :, reqs:].reshape(cols, rows, padded, width)
+    rec_all = rec_all[:, :, :rec_toks * reqs]
 
     def by_cell(table):
         table = table.reshape(reqs, rows, cols, rec_toks).transpose(2, 1, 3, 0)
@@ -417,9 +597,6 @@
     cache = jnp.where(replaced, placed, stale_here)
     cache = cache.reshape(reqs, heads_here, num_patches, PLEN, 2 * HD)
 
-    entering = hidden.transpose(0, 2, 1, 3)
-    out_rows = out_weight[0].reshape(rows, heads_here * HD, width)
-    my_offsets = (row * cols + col) * toks + jnp.arange(toks, dtype=jnp.int32)
     cell = jnp.reshape(row, (1,)).astype(jnp.int32)
     leavings = []
     incoming = entering[0]
@@ -430,12 +607,16 @@
             inputs = incoming
         else:
             inputs = jnp.where(section == 0, entering[turn], incoming)
-        normed = modulate_split(inputs, my_positions, modulation)
+        if turn == 0:
+            tokens = first_all[:, :, :reqs]
+        else:
+            normed = modulate_split(inputs, my_positions, modulation)
+            tokens = gather_tokens(normed, rows, cols, 1)
         cache, attended = block_call(
-            patch.reshape(1), cell, gather_cells(normed), qkv_weight, gains, cosine, sine, bias,
+            patch.reshape(1), cell, tokens, qkv_weight, gains, cosine, sine, bias,
             cache,
         )
-        returned = lax.all_to_all(attended, "row", 0, 0, tiled=True)
+        returned = exchange_rows(attended, 2)
         returned = returned.transpose(1, 2, 3, 0, 4).reshape(cols * reqs * toks, -1)
         partial = jnp.dot(
             returned, out_weight[0], preferred_element_type=jnp.float32

time: 811 us -> 726 us (0.90)
  Pallas kernels: 117 us -> 424 us
  waiting for transfers between devices: 388 us -> 86.3 us
  blocking collectives: 139 us -> 14.2 us
  matrix products: 22.2 us -> 46.7 us
  local copies, waits for them, and re-layouts: 76.7 us -> 100 us
  between operations: 15.4 us -> 2.5 us
    pallas_call x0 -> x14, Pallas kernels: none -> 307 us  [the longest x7 229 us: gather_tokens(): pl.pallas_call(gather_body, out_shape=jax.ShapeDtypeStruct((cols, rows) +...]
    all_gather x15 -> x0, waiting for transfers between devices: 294 us -> none  [gather_cells(): return lax.all_gather(lax.all_gather(value, 'row', axis=0), 'col', axis=0)]
    all_to_all x6 -> x0, blocking collectives: 99.9 us -> none  [local_split(): returned = lax.all_to_all(attended, 'row', 0, 0, tiled=True)]
    all_gather x1 -> x0, blocking collectives: 24.4 us -> none  [gather_cells(): return lax.all_gather(lax.all_gather(value, 'row', axis=0), 'col', axis=0)]
    dot_general x7, matrix products: 13.6 us -> 36.4 us  [local_split(): jnp.dot(returned, out_weight[0], preferred_element_type=jnp.float32)]
    all_to_all x1 -> x0, waiting for transfers between devices: 11.4 us -> none  [local_split(): returned = lax.all_to_all(attended, 'row', 0, 0, tiled=True)]
    unnamed x113 -> x101, local copies, waits for them, and re-layouts: 22 us -> 29.1 us
    dot_general x2 -> x3, local copies, waits for them, and re-layouts: 16.9 us -> 18.4 us  [local_split(): jnp.dot(rec_all.reshape(-1, width), weights_here, preferred_element_type=...]
  transfers between devices with their start and end apart: 29 -> 13, of which waited for: 26 -> 13; matrix products, arithmetic and copies ran while one was open for 8% -> 0% of each run, Pallas kernels for 0% -> 0%
where the time goes in v2:
time: 726 us; the launch traced here: 718 us
  Pallas kernels  424 us (58%)
  local copies, waits for them, and re-layouts  100 us (14%)
  waiting for transfers between devices  86.3 us (12%)
  matrix products  46.7 us (6%)
  other arithmetic  35.7 us (5%)
  blocking collectives  14.2 us (2%)
  starting transfers between devices  8.11 us (1%)
    pallas_call x7, Pallas kernels, gather_tokens(): pl.pallas_call(gather_body, out_shape=jax.ShapeDtypeStruct((cols, rows) +...  229 us
    pallas_call x7, Pallas kernels, block_call(): pl.pallas_call(block_body, grid_spec=grid_spec, out_shape=[jax.ShapeDtype...  116 us
    pallas_call x7, Pallas kernels, exchange_rows(): pl.pallas_call(exchange_body, out_shape=jax.ShapeDtypeStruct(value.shape,...  78.2 us
    ppermute x6, waiting for transfers between devices, passed_along(): return lax.ppermute(value, axis, pairs)  74 us
    dot_general x7, matrix products, local_split(): jnp.dot(returned, out_weight[0], preferred_element_type=jnp.float32)  36.4 us
    unnamed x101, local copies, waits for them, and re-layouts  29.1 us
    dot_general x3, local copies, waits for them, and re-layouts, local_split(): jnp.dot(rec_all.reshape(-1, width), weights_here, preferred_element_type=...  18.4 us
  transfers between devices with their start and end apart: 13, of which 13 were waited for; matrix products, arithmetic and copies ran while one was open for 0% of the time, Pallas kernels for 0%

profile of v2, /device:TPU:6, one launch (start us, length us, event | category | flops | bytes accessed | tf_op | source)
XLA Modules:
  0.0 717.7 jit_solution(8213555080812291660)
XLA Ops:
  6.4 14.2 %all-gather = f32[8,1,2304]{2,1,0:T(1,128)S(1)} all-gather(f32[1,1,2304]{2,1,0:T(1,128)S(1)} %convolution_bitcast_fusion), channel_id=1, replica_groups=mesh['section'=4,'row'=4,'col'=2] {'row','col'}, dimensions={0}, use_global_device_ids=true | all-gather | bytes 82944 | tf_op jit(solution)/shard_map/all_gather | solution.py:542
  29.3 43.3 %shard_map.109 = bf16[2,4,3,32,3072]{4,3,2,1,0:T(8,128)(2,1)} custom-call(bf16[3,32,3072]{2,1,0:T(8,128)(2,1)} %pad_maximum_fusion.3.x_ref), custom_call_target="tpu_custom_call" | custom-call | bytes 41943040 | tf_op jit(solution)/shard_map/pallas_call | solution.py:453
  143.0 16.5 %shard_map.110 = (bf16[2,6,4,256,128]{4,3,2,1,0:T(8,128)(2,1)S(1)}, bf16[4,2,2,32,384]{4,3,2,1,0:T(8,128)(2,1)S(1)}) custom-call(s32[1]{0:T(128)} %bitcast.6.patch_ref, s32[1]{0:T(128)} %bitcast.7.cell_ref, bf16[2,4,2,32,3072]{4,3,2,1,0:T(8,128)(2,1)S(1)} %copy-done.2, bf16[1,3072,4608]{2,1,0:T(8,128)(2,1)} %w_ref.13, ...), custom_call_target="tpu_custom_call" | custom-call | flops 5234491392 | bytes 20971520 | tf_op jit(solution)/shard_map/pallas_call | solution.py:316
  185.7 12.0 %collective-permute-done.1 = bf16[2,32,3072]{2,1,0:T(8,128)(2,1)S(1)} collective-permute-done((bf16[2,32,3072]{2,1,0:T(8,128)(2,1)}, bf16[2,32,3072]{2,1,0:T(8,128)(2,1)S(1)}, u32[]{:S(2)}, u32[]{:S(2)}) %collective-permute-start.1) | collective-permute-done | bytes 393248 | tf_op jit(solution)/shard_map/ppermute | solution.py:18
  200.2 31.0 %shard_map.112.x_ref = bf16[2,4,2,32,3072]{4,3,2,1,0:T(8,128)(2,1)} custom-call(bf16[2,32,3072]{2,1,0:T(8,128)(2,1)} %fusion.77.x_ref), custom_call_target="tpu_custom_call" | custom-call | bytes 41943040 | tf_op jit(solution)/shard_map/pallas_call | solution.py:453
  233.1 16.7 %shard_map.113 = (bf16[2,6,4,256,128]{4,3,2,1,0:T(8,128)(2,1)S(1)}, bf16[4,2,2,32,384]{4,3,2,1,0:T(8,128)(2,1)S(1)}) custom-call(s32[1]{0:T(128)} %bitcast.66.patch_ref, s32[1]{0:T(128)} %bitcast.7.cell_ref, bf16[2,4,2,32,3072]{4,3,2,1,0:T(8,128)(2,1)S(1)} %copy-done.4, bf16[1,3072,4608]{2,1,0:T(8,128)(2,1)} %w_ref.13, ...), custom_call_target="tpu_custom_call" | custom-call | flops 5234491392 | bytes 20971520 | tf_op jit(solution)/shard_map/pallas_call | solution.py:316
  274.0 11.8 %collective-permute-done.3 = bf16[2,32,3072]{2,1,0:T(8,128)(2,1)S(1)} collective-permute-done((bf16[2,32,3072]{2,1,0:T(8,128)(2,1)S(1)}, bf16[2,32,3072]{2,1,0:T(8,128)(2,1)S(1)}, u32[]{:S(2)}, u32[]{:S(2)}) %collective-permute-start.3) | collective-permute-done | bytes 393248 | tf_op jit(solution)/shard_map/ppermute | solution.py:18
  288.3 31.0 %shard_map.115.x_ref = bf16[2,4,2,32,3072]{4,3,2,1,0:T(8,128)(2,1)} custom-call(bf16[2,32,3072]{2,1,0:T(8,128)(2,1)} %fusion.73.x_ref), custom_call_target="tpu_custom_call" | custom-call | bytes 41943040 | tf_op jit(solution)/shard_map/pallas_call | solution.py:453
  321.2 16.4 %shard_map.116 = (bf16[2,6,4,256,128]{4,3,2,1,0:T(8,128)(2,1)S(1)}, bf16[4,2,2,32,384]{4,3,2,1,0:T(8,128)(2,1)S(1)}) custom-call(s32[1]{0:T(128)} %bitcast.74.patch_ref, s32[1]{0:T(128)} %bitcast.7.cell_ref, bf16[2,4,2,32,3072]{4,3,2,1,0:T(8,128)(2,1)S(1)} %copy-done.5, bf16[1,3072,4608]{2,1,0:T(8,128)(2,1)} %w_ref.13, ...), custom_call_target="tpu_custom_call" | custom-call | flops 5234491392 | bytes 20971520 | tf_op jit(solution)/shard_map/pallas_call | solution.py:316
  361.9 12.3 %collective-permute-done.5 = bf16[2,32,3072]{2,1,0:T(8,128)(2,1)S(1)} collective-permute-done((bf16[2,32,3072]{2,1,0:T(8,128)(2,1)S(1)}, bf16[2,32,3072]{2,1,0:T(8,128)(2,1)S(1)}, u32[]{:S(2)}, u32[]{:S(2)}) %collective-permute-start.5) | collective-permute-done | bytes 393248 | tf_op jit(solution)/shard_map/ppermute | solution.py:18
  376.8 31.0 %shard_map.118.x_ref = bf16[2,4,2,32,3072]{4,3,2,1,0:T(8,128)(2,1)} custom-call(bf16[2,32,3072]{2,1,0:T(8,128)(2,1)} %fusion.69.x_ref), custom_call_target="tpu_custom_call" | custom-call | bytes 41943040 | tf_op jit(solution)/shard_map/pallas_call | solution.py:453
  409.7 16.4 %shard_map.119 = (bf16[2,6,4,256,128]{4,3,2,1,0:T(8,128)(2,1)S(1)}, bf16[4,2,2,32,384]{4,3,2,1,0:T(8,128)(2,1)S(1)}) custom-call(s32[1]{0:T(128)} %bitcast.82.patch_ref, s32[1]{0:T(128)} %bitcast.7.cell_ref, bf16[2,4,2,32,3072]{4,3,2,1,0:T(8,128)(2,1)S(1)} %copy-done.6, bf16[1,3072,4608]{2,1,0:T(8,128)(2,1)} %w_ref.13, ...), custom_call_target="tpu_custom_call" | custom-call | flops 5234491392 | bytes 20971520 | tf_op jit(solution)/shard_map/pallas_call | solution.py:316
  428.5 11.2 %shard_map.120 = bf16[4,2,2,32,384]{4,3,2,1,0:T(8,128)(2,1)} custom-call(bf16[4,2,2,32,384]{4,3,2,1,0:T(8,128)(2,1)} %copy-done.19), custom_call_target="tpu_custom_call" | custom-call | bytes 16777216 | tf_op jit(solution)/shard_map/pallas_call | solution.py:497
  450.4 12.6 %collective-permute-done.7 = bf16[2,32,3072]{2,1,0:T(8,128)(2,1)S(1)} collective-permute-done((bf16[2,32,3072]{2,1,0:T(8,128)(2,1)S(1)}, bf16[2,32,3072]{2,1,0:T(8,128)(2,1)S(1)}, u32[]{:S(2)}, u32[]{:S(2)}) %collective-permute-start.7) | collective-permute-done | bytes 393248 | tf_op jit(solution)/shard_map/ppermute | solution.py:18
  464.5 31.0 %shard_map.121.x_ref = bf16[2,4,2,32,3072]{4,3,2,1,0:T(8,128)(2,1)} custom-call(bf16[2,32,3072]{2,1,0:T(8,128)(2,1)} %fusion.65.x_ref), custom_call_target="tpu_custom_call" | custom-call | bytes 41943040 | tf_op jit(solution)/shard_map/pallas_call | solution.py:453
  497.4 16.5 %shard_map.122 = (bf16[2,6,4,256,128]{4,3,2,1,0:T(8,128)(2,1)S(1)}, bf16[4,2,2,32,384]{4,3,2,1,0:T(8,128)(2,1)S(1)}) custom-call(s32[1]{0:T(128)} %bitcast.89.patch_ref, s32[1]{0:T(128)} %bitcast.7.cell_ref, bf16[2,4,2,32,3072]{4,3,2,1,0:T(8,128)(2,1)S(1)} %copy-done.7, bf16[1,3072,4608]{2,1,0:T(8,128)(2,1)} %w_ref.13, ...), custom_call_target="tpu_custom_call" | custom-call | flops 5234491392 | bytes 20971520 | tf_op jit(solution)/shard_map/pallas_call | solution.py:316
  538.2 12.7 %collective-permute-done.9 = bf16[2,32,3072]{2,1,0:T(8,128)(2,1)S(1)} collective-permute-done((bf16[2,32,3072]{2,1,0:T(8,128)(2,1)S(1)}, bf16[2,32,3072]{2,1,0:T(8,128)(2,1)S(1)}, u32[]{:S(2)}, u32[]{:S(2)}) %collective-permute-start.9) | collective-permute-done | bytes 393248 | tf_op jit(solution)/shard_map/ppermute | solution.py:18
  552.3 31.0 %shard_map.124.x_ref = bf16[2,4,2,32,3072]{4,3,2,1,0:T(8,128)(2,1)} custom-call(bf16[2,32,3072]{2,1,0:T(8,128)(2,1)} %fusion.61.x_ref), custom_call_target="tpu_custom_call" | custom-call | bytes 41943040 | tf_op jit(solution)/shard_map/pallas_call | solution.py:453
  585.2 16.5 %shard_map.125 = (bf16[2,6,4,256,128]{4,3,2,1,0:T(8,128)(2,1)S(1)}, bf16[4,2,2,32,384]{4,3,2,1,0:T(8,128)(2,1)S(1)}) custom-call(s32[1]{0:T(128)} %bitcast.96.patch_ref, s32[1]{0:T(128)} %bitcast.7.cell_ref, bf16[2,4,2,32,3072]{4,3,2,1,0:T(8,128)(2,1)S(1)} %copy-done.8, bf16[1,3072,4608]{2,1,0:T(8,128)(2,1)} %w_ref.13, ...), custom_call_target="tpu_custom_call" | custom-call | flops 5234491392 | bytes 20971520 | tf_op jit(solution)/shard_map/pallas_call | solution.py:316
  604.1 11.2 %shard_map.126 = bf16[4,2,2,32,384]{4,3,2,1,0:T(8,128)(2,1)} custom-call(bf16[4,2,2,32,384]{4,3,2,1,0:T(8,128)(2,1)} %copy-done.21), custom_call_target="tpu_custom_call" | custom-call | bytes 16777216 | tf_op jit(solution)/shard_map/pallas_call | solution.py:497
  626.0 12.7 %collective-permute-done.11 = bf16[2,32,3072]{2,1,0:T(8,128)(2,1)S(1)} collective-permute-done((bf16[2,32,3072]{2,1,0:T(8,128)(2,1)S(1)}, bf16[2,32,3072]{2,1,0:T(8,128)(2,1)S(1)}, u32[]{:S(2)}, u32[]{:S(2)}) %collective-permute-start.11) | collective-permute-done | bytes 393248 | tf_op jit(solution)/shard_map/ppermute | solution.py:18
  640.2 31.0 %shard_map.127.x_ref = bf16[2,4,2,32,3072]{4,3,2,1,0:T(8,128)(2,1)} custom-call(bf16[2,32,3072]{2,1,0:T(8,128)(2,1)} %fusion.57.x_ref), custom_call_target="tpu_custom_call" | custom-call | bytes 41943040 | tf_op jit(solution)/shard_map/pallas_call | solution.py:453
  673.0 17.3 %shard_map.128 = (bf16[2,6,4,256,128]{4,3,2,1,0:T(8,128)(2,1)}, bf16[4,2,2,32,384]{4,3,2,1,0:T(8,128)(2,1)S(1)}) custom-call(s32[1]{0:T(128)} %bitcast.103.patch_ref, s32[1]{0:T(128)} %bitcast.7.cell_ref, bf16[2,4,2,32,3072]{4,3,2,1,0:T(8,128)(2,1)S(1)} %copy-done.3, bf16[1,3072,4608]{2,1,0:T(8,128)(2,1)} %w_ref.13, ...), custom_call_target="tpu_custom_call" | custom-call | flops 5234491392 | bytes 20971520 | tf_op jit(solution)/shard_map/pallas_call | solution.py:316
  691.1 11.2 %shard_map.129 = bf16[4,2,2,32,384]{4,3,2,1,0:T(8,128)(2,1)} custom-call(bf16[4,2,2,32,384]{4,3,2,1,0:T(8,128)(2,1)} %copy-done.15), custom_call_target="tpu_custom_call" | custom-call | bytes 16777216 | tf_op jit(solution)/shard_map/pallas_call | solution.py:497
  (303 shorter events, 247.8 us)
Async XLA Ops:
  0.0 24.3 %copy-start.29 = (s32[1024]{0:T(1024)}, s32[1024]{0:T(1024)S(1)}, u32[]{:S(2)}) copy-start(s32[1024]{0:T(1024)S(1)} %add_select_fusion.5) | copy-start | bytes 12292
  5.1 16.3 %copy-start.31 = (s32[2,96]{1,0:T(2,128)S(1)}, s32[2,96]{1,0:T(2,128)}, u32[]{:S(2)}) copy-start(s32[2,96]{1,0:T(2,128)} %param.21) | copy-start | bytes 2308
  20.6 603.2 %copy-start.27 = (f32[3072]{0:T(1024)}, f32[3072]{0:T(1024)S(1)}, u32[]{:S(2)}) copy-start(f32[3072]{0:T(1024)S(1)} %get-tuple-element.60) | copy-start | bytes 36868
  24.3 48.3 %copy-start.23 = (s32[1024,2]{1,0:T(8,128)}, s32[1024,2]{1,0:T(8,128)S(1)}, u32[]{:S(2)}) copy-start(s32[1024,2]{1,0:T(8,128)S(1)} %gather_fusion) | copy-start | bytes 24580
  107.6 16.2 %copy-start.33 = (f32[64]{0:T(128)}, f32[64]{0:T(128)S(1)}, u32[]{:S(2)}) copy-start(f32[64]{0:T(128)S(1)} %get-tuple-element.88) | copy-start | bytes 772
  179.5 19.6 %copy-start.40 = (pred[2,32]{1,0:T(4,128)(4,1)S(1)}, pred[2,32]{1,0:T(4,128)(4,1)}, u32[]{:S(2)}) copy-start(pred[2,32]{1,0:T(4,128)(4,1)} %get-tuple-element.92) | copy-start | bytes 196
  180.3 1.9 collective-permute-start
  184.4 13.2 %collective-permute-start.1 = (bf16[2,32,3072]{2,1,0:T(8,128)(2,1)}, bf16[2,32,3072]{2,1,0:T(8,128)(2,1)S(1)}, u32[]{:S(2)}, u32[]{:S(2)}) collective-permute-start(bf16[2,32,3072]{2,1,0:T(8,128)(2,1)} %get-tuple-element.48), channel_id=1, source_target_pairs={{0,8},{8,16},{16,24},{1,9},{9,17},{17,25},{2,10},{10,18},{18,26},{... | collective-permute-start | bytes 1179656 | tf_op jit(solution)/shard_map/ppermute | solution.py:18
  269.9 17.3 %copy-start.39 = (pred[2,32]{1,0:T(4,128)(4,1)S(1)}, pred[2,32]{1,0:T(4,128)(4,1)}, u32[]{:S(2)}) copy-start(pred[2,32]{1,0:T(4,128)(4,1)} %get-tuple-element.93) | copy-start | bytes 196
  270.0 1.8 collective-permute-start.2
  272.8 13.0 %collective-permute-start.3 = (bf16[2,32,3072]{2,1,0:T(8,128)(2,1)S(1)}, bf16[2,32,3072]{2,1,0:T(8,128)(2,1)S(1)}, u32[]{:S(2)}, u32[]{:S(2)}) collective-permute-start(bf16[2,32,3072]{2,1,0:T(8,128)(2,1)S(1)} %get-tuple-element.44), channel_id=1, source_target_pairs={{0,8},{8,16},{16,24},{1,9},{9,17},{17,25},{2,10},{10,18},{18,26},{... | collective-permute-start | bytes 1179656 | tf_op jit(solution)/shard_map/ppermute | solution.py:18
  357.8 17.9 %copy-start.38 = (pred[2,32]{1,0:T(4,128)(4,1)S(1)}, pred[2,32]{1,0:T(4,128)(4,1)}, u32[]{:S(2)}) copy-start(pred[2,32]{1,0:T(4,128)(4,1)} %get-tuple-element.94) | copy-start | bytes 196
  357.8 1.8 collective-permute-start.4
  360.6 13.6 %collective-permute-start.5 = (bf16[2,32,3072]{2,1,0:T(8,128)(2,1)S(1)}, bf16[2,32,3072]{2,1,0:T(8,128)(2,1)S(1)}, u32[]{:S(2)}, u32[]{:S(2)}) collective-permute-start(bf16[2,32,3072]{2,1,0:T(8,128)(2,1)S(1)} %get-tuple-element.40), channel_id=1, source_target_pairs={{0,8},{8,16},{16,24},{1,9},{9,17},{17,25},{2,10},{10,18},{18,26},{... | collective-permute-start | bytes 1179656 | tf_op jit(solution)/shard_map/ppermute | solution.py:18
  446.3 17.2 %copy-start.37 = (pred[2,32]{1,0:T(4,128)(4,1)S(1)}, pred[2,32]{1,0:T(4,128)(4,1)}, u32[]{:S(2)}) copy-start(pred[2,32]{1,0:T(4,128)(4,1)} %get-tuple-element.95) | copy-start | bytes 196
  446.3 1.8 collective-permute-start.6
  449.1 13.9 %collective-permute-start.7 = (bf16[2,32,3072]{2,1,0:T(8,128)(2,1)S(1)}, bf16[2,32,3072]{2,1,0:T(8,128)(2,1)S(1)}, u32[]{:S(2)}, u32[]{:S(2)}) collective-permute-start(bf16[2,32,3072]{2,1,0:T(8,128)(2,1)S(1)} %get-tuple-element.36), channel_id=1, source_target_pairs={{0,8},{8,16},{16,24},{1,9},{9,17},{17,25},{2,10},{10,18},{18,26},{... | collective-permute-start | bytes 1179656 | tf_op jit(solution)/shard_map/ppermute | solution.py:18
  534.1 17.2 %copy-start.36 = (pred[2,32]{1,0:T(4,128)(4,1)S(1)}, pred[2,32]{1,0:T(4,128)(4,1)}, u32[]{:S(2)}) copy-start(pred[2,32]{1,0:T(4,128)(4,1)} %get-tuple-element.96) | copy-start | bytes 196
  534.1 1.8 collective-permute-start.8
  536.9 13.9 %collective-permute-start.9 = (bf16[2,32,3072]{2,1,0:T(8,128)(2,1)S(1)}, bf16[2,32,3072]{2,1,0:T(8,128)(2,1)S(1)}, u32[]{:S(2)}, u32[]{:S(2)}) collective-permute-start(bf16[2,32,3072]{2,1,0:T(8,128)(2,1)S(1)} %get-tuple-element.34), channel_id=1, source_target_pairs={{0,8},{8,16},{16,24},{1,9},{9,17},{17,25},{2,10},{10,18},{18,26},{... | collective-permute-start | bytes 1179656 | tf_op jit(solution)/shard_map/ppermute | solution.py:18
  621.9 17.2 %copy-start.35 = (pred[2,32]{1,0:T(4,128)(4,1)S(1)}, pred[2,32]{1,0:T(4,128)(4,1)}, u32[]{:S(2)}) copy-start(pred[2,32]{1,0:T(4,128)(4,1)} %get-tuple-element.90) | copy-start | bytes 196
  622.0 1.8 collective-permute-start.10
  624.8 13.9 %collective-permute-start.11 = (bf16[2,32,3072]{2,1,0:T(8,128)(2,1)S(1)}, bf16[2,32,3072]{2,1,0:T(8,128)(2,1)S(1)}, u32[]{:S(2)}, u32[]{:S(2)}) collective-permute-start(bf16[2,32,3072]{2,1,0:T(8,128)(2,1)S(1)} %get-tuple-element.32), channel_id=1, source_target_pairs={{0,8},{8,16},{16,24},{1,9},{9,17},{17,25},{2,10},{10,18},{18,26},{... | collective-permute-start | bytes 1179656 | tf_op jit(solution)/shard_map/ppermute | solution.py:18
  708.8 1.9 collective-permute-start.12
  (35 other events, 121.7 us)

commit v3 on v2

--- a/solution.py
+++ b/solution.py
@@ -336,120 +336,78 @@
     return (normed * (1.0 + scales) + shifts).astype(jnp.bfloat16)
 
 
-def gather_body(x_ref, out_ref, own_sem, line_send, line_recv, side_send, side_recv):
+def gather_body(x_ref, out_ref, own_sem, line_send, line_recv, far_send, far_recv, side_send,
+                side_recv):
     chunks = x_ref.shape[0]
     rows = out_ref.shape[1]
     w = lax.axis_index("row")
     c = lax.axis_index("col")
-    sibling = {"col": 1 - c}
+    above = lax.rem(w + 1, rows)
+    below = lax.rem(w + rows - 1, rows)
+    across = lax.rem(w + 2, rows)
     barrier = pltpu.get_barrier_semaphore()
-    has = {1: w < rows - 1, -1: w > 0}
-
-    def greet(way):
-        @pl.when(has[way])
-        def _():
-            pl.semaphore_signal(barrier, inc=1, device_id={"row": w + way},
-                                device_id_type=pl.DeviceIdType.MESH)
-
-    pl.semaphore_signal(barrier, inc=1, device_id=sibling, device_id_type=pl.DeviceIdType.MESH)
-    greet(1)
-    greet(-1)
-    inside = has[1] & has[-1]
-
-    @pl.when(inside)
-    def _():
-        pl.semaphore_wait(barrier, 3)
-
-    @pl.when(jnp.logical_not(inside))
-    def _():
-        pl.semaphore_wait(barrier, 2)
-
-    def line_copy(way, step, chunk):
-        block = w - way * step
-        source = x_ref.at[chunk] if step == 0 else out_ref.at[c, block, chunk]
-        lane = 0 if way == 1 else 1
+    for peer in ({"col": 1 - c}, {"row": above}, {"row": below}):
+        pl.semaphore_signal(barrier, inc=1, device_id=peer, device_id_type=pl.DeviceIdType.MESH)
+    pl.semaphore_wait(barrier, 3)
+
+    def sent(source, core, block, chunk, send, receive, peer):
         return pltpu.make_async_remote_copy(
-            src_ref=source, dst_ref=out_ref.at[c, block, chunk],
-            send_sem=line_send.at[lane, step, chunk], recv_sem=line_recv.at[lane, step, chunk],
-            device_id={"row": w + way}, device_id_type=pl.DeviceIdType.MESH,
-        )
-
-    def arrival(way, step, chunk):
-        block = w - way * (step + 1)
-        lane = 0 if way == 1 else 1
-        return pltpu.make_async_remote_copy(
-            src_ref=x_ref.at[chunk], dst_ref=out_ref.at[c, block, chunk],
-            send_sem=line_send.at[lane, step, chunk], recv_sem=line_recv.at[lane, step, chunk],
-            device_id={"row": w + way}, device_id_type=pl.DeviceIdType.MESH,
-        )
-
-    def side_copy(place, block, chunk):
+            src_ref=source, dst_ref=out_ref.at[core, block, chunk], send_sem=send,
+            recv_sem=receive, device_id=peer, device_id_type=pl.DeviceIdType.MESH,
+        )
+
+    targets = ({"row": above}, {"row": below})
+    arriving = (below, above)
+
+    def near(lane, chunk, block):
+        return sent(x_ref.at[chunk], c, block, chunk, line_send.at[lane, chunk],
+                    line_recv.at[lane, chunk], targets[lane])
+
+    def far(chunk, block):
+        lane = chunk % 2
+        return sent(out_ref.at[c, arriving[lane], chunk], c, block, chunk, far_send.at[chunk],
+                    far_recv.at[chunk], targets[lane])
+
+    def side(place, chunk, core, block):
         source = x_ref.at[chunk] if place == 0 else out_ref.at[c, block, chunk]
-        return pltpu.make_async_remote_copy(
-            src_ref=source, dst_ref=out_ref.at[c, block, chunk],
-            send_sem=side_send.at[place, chunk], recv_sem=side_recv.at[place, chunk],
-            device_id=sibling, device_id_type=pl.DeviceIdType.MESH,
-        )
-
-    def side_arrival(place, block, chunk):
-        return pltpu.make_async_remote_copy(
-            src_ref=x_ref.at[chunk], dst_ref=out_ref.at[1 - c, block, chunk],
-            send_sem=side_send.at[place, chunk], recv_sem=side_recv.at[place, chunk],
-            device_id=sibling, device_id_type=pl.DeviceIdType.MESH,
-        )
-
-    def arrives(way, step):
-        return w >= step + 1 if way == 1 else w <= rows - 2 - step
-
-    def leaves(way, step):
-        held = w >= step if way == 1 else w <= rows - 1 - step
-        return has[way] & held
-
-    def place_of(way, step):
-        return 1 + step if way == 1 else rows + step
-
+        return sent(source, core, block, chunk, side_send.at[place, chunk],
+                    side_recv.at[place, chunk], {"col": 1 - c})
+
+    for first in (0, 1):
+        for chunk in range(chunks):
+            for lane in (0, 1):
+                if (chunk % 2 == lane) == (first == 0):
+                    near(lane, chunk, w).start()
+    kept = []
     for chunk in range(chunks):
-        for way in (1, -1):
-            @pl.when(leaves(way, 0))
-            def _():
-                line_copy(way, 0, chunk).start()
-    own = []
+        side(0, chunk, c, w).start()
+        copy = pltpu.make_async_copy(x_ref.at[chunk], out_ref.at[c, w, chunk], own_sem.at[chunk])
+        copy.start()
+        kept.append(copy)
     for chunk in range(chunks):
-        side_copy(0, w, chunk).start()
-        kept = pltpu.make_async_copy(x_ref.at[chunk], out_ref.at[c, w, chunk], own_sem.at[chunk])
-        kept.start()
-        own.append(kept)
-    for step in range(rows - 1):
-        for chunk in range(chunks):
-            for way in (1, -1):
-                @pl.when(arrives(way, step))
-                def _():
-                    arrival(way, step, chunk).wait_recv()
-                    if step + 1 < rows - 1:
-                        @pl.when(leaves(way, step + 1))
-                        def _():
-                            line_copy(way, step + 1, chunk).start()
-                    side_copy(place_of(way, step), w - way * (step + 1), chunk).start()
+        lane = chunk % 2
+        near(lane, chunk, arriving[lane]).wait_recv()
+        far(chunk, arriving[lane]).start()
+        side(1 + lane, chunk, c, arriving[lane]).start()
     for chunk in range(chunks):
-        own[chunk].wait()
-        side_copy(0, w, chunk).wait_send()
-        side_arrival(0, w, chunk).wait_recv()
-        for step in range(rows - 1):
-            for way in (1, -1):
-                @pl.when(leaves(way, step))
-                def _():
-                    line_copy(way, step, chunk).wait_send()
-
-                @pl.when(arrives(way, step))
-                def _():
-                    block = w - way * (step + 1)
-                    side_copy(place_of(way, step), block, chunk).wait_send()
-                    side_arrival(place_of(way, step), block, chunk).wait_recv()
+        lane = 1 - chunk % 2
+        near(lane, chunk, arriving[lane]).wait_recv()
+        side(1 + lane, chunk, c, arriving[lane]).start()
+    for chunk in range(chunks):
+        far(chunk, across).wait_recv()
+        side(3, chunk, c, across).start()
+    for chunk in range(chunks):
+        kept[chunk].wait()
+        far(chunk, across).wait_send()
+        for lane in (0, 1):
+            near(lane, chunk, w).wait_send()
+        for place, block in enumerate((w, below, above, across)):
+            side(place, chunk, c, block).wait_send()
+            side(place, chunk, 1 - c, block).wait_recv()
 
 
 def gather_tokens(value, rows, cols, number):
     chunks = value.shape[0]
-    steps = rows - 1
     return pl.pallas_call(
         gather_body,
         out_shape=jax.ShapeDtypeStruct((cols, rows) + value.shape, value.dtype),
@@ -457,14 +415,38 @@
         out_specs=pl.BlockSpec(memory_space=pl.ANY),
         scratch_shapes=[
             pltpu.SemaphoreType.DMA((chunks,)),
-            pltpu.SemaphoreType.DMA((2, steps, chunks)),
-            pltpu.SemaphoreType.DMA((2, steps, chunks)),
-            pltpu.SemaphoreType.DMA((2 * steps + 1, chunks)),
-            pltpu.SemaphoreType.DMA((2 * steps + 1, chunks)),
+            pltpu.SemaphoreType.DMA((2, chunks)),
+            pltpu.SemaphoreType.DMA((2, chunks)),
+            pltpu.SemaphoreType.DMA((chunks,)),
+            pltpu.SemaphoreType.DMA((chunks,)),
+            pltpu.SemaphoreType.DMA((4, chunks)),
+            pltpu.SemaphoreType.DMA((4, chunks)),
         ],
         compiler_params=pltpu.CompilerParams(collective_id=number, has_side_effects=True),
         cost_estimate=pl.CostEstimate(flops=0, bytes_accessed=40 * 1024 * 1024, transcendentals=0),
     )(value)
+
+
+def project_body(cell_ref, x_ref, w_ref, out_ref):
+    out_ref[...] = jnp.dot(x_ref[...], w_ref[0], preferred_element_type=jnp.float32)
+
+
+def project_call(cell, x, weights, pair_count):
+    count, width = x.shape
+    return pl.pallas_call(
+        project_body,
+        grid_spec=pltpu.PrefetchScalarGridSpec(
+            num_scalar_prefetch=1,
+            grid=(pair_count,),
+            in_specs=[
+                pl.BlockSpec((count, width), lambda j, m: (0, 0)),
+                pl.BlockSpec((1, width, HEAD_PAIR), lambda j, m: (0, 0, m[0] * pair_count + j)),
+            ],
+            out_specs=pl.BlockSpec((count, HEAD_PAIR), lambda j, m: (0, j)),
+        ),
+        out_shape=jax.ShapeDtypeStruct((count, HEAD_PAIR * pair_count), jnp.float32),
+        compiler_params=pltpu.CompilerParams(vmem_limit_bytes=24 * 1024 * 1024),
+    )(cell, x, weights)
 
 
 def exchange_body(x_ref, out_ref, own_sem, send_sem, recv_sem):
@@ -539,7 +521,8 @@
 
     embedding = jax.nn.silu(time_table[timestep[0]]).astype(jnp.bfloat16)
     mod_part = jnp.dot(embedding, ada_weight[0], preferred_element_type=jnp.float32)
-    modulation = lax.all_gather(mod_part, ("row", "col"), axis=0, tiled=True).reshape(6, width)
+    mod_all = gather_tokens(jnp.broadcast_to(mod_part, (1, 8) + mod_part.shape), rows, cols, 3)
+    modulation = mod_all[:, :, 0, 0].transpose(1, 0, 2).reshape(6, width)
 
     cell_positions = positions.reshape(reqs, num_patches, rows, cols, toks)
     cell_positions = cell_positions.transpose(1, 3, 2, 0, 4).reshape(num_patches, -1)
@@ -580,11 +563,9 @@
 
     rec_places = by_cell(rec_positions)
     rec_slots = by_cell(recompute_slots)
-    per_row = heads_here * 3 * HD
-    weights_here = lax.dynamic_slice_in_dim(qkv_weight[0], row * per_row, per_row, 1)
-    rec_mixed = jnp.dot(
-        rec_all.reshape(-1, width), weights_here, preferred_element_type=jnp.float32
-    ).reshape(rec, reqs, heads_here, 3, HD)
+    cell = jnp.reshape(row, (1,)).astype(jnp.int32)
+    rec_mixed = project_call(cell, rec_all.reshape(-1, width), qkv_weight, heads_here // 2)
+    rec_mixed = rec_mixed.reshape(rec, reqs, heads_here, 3, HD)
     rec_pairs = heads_from(rec_mixed, rec_places, qk_gain[0])[..., HD:]
     stale_here = lax.dynamic_slice_in_dim(stale_kv[0], row * heads_here, heads_here, 2)
     stale_here = stale_here.transpose(1, 2, 0, 3)
@@ -597,7 +578,6 @@
     cache = jnp.where(replaced, placed, stale_here)
     cache = cache.reshape(reqs, heads_here, num_patches, PLEN, 2 * HD)
 
-    cell = jnp.reshape(row, (1,)).astype(jnp.int32)
     leavings = []
     incoming = entering[0]
     for turn in range(num_patches + section_count - 1):
@@ -638,7 +618,7 @@
 
 def fits_split(mesh):
     heads = 48 // mesh.shape["col"]
-    return mesh.shape["col"] == 2 and heads % (2 * mesh.shape["row"]) == 0
+    return mesh.shape["col"] == 2 and mesh.shape["row"] == 4 and heads % (2 * mesh.shape["row"]) == 0
 
 
 def solution(mesh):

time: 726 us -> 748 us (1.030)
  Pallas kernels: 424 us -> 448 us
  blocking collectives: 14.2 us -> 0 us
  other arithmetic: 35.7 us -> 44.7 us
    dot_general x3 -> x0, local copies, waits for them, and re-layouts: 18.4 us -> none  [local_split(): jnp.dot(rec_all.reshape(-1, width), weights_here, preferred_element_type=...]
    pallas_call x7 -> x8, Pallas kernels: 229 us -> 244 us  [gather_tokens(): pl.pallas_call(gather_body, out_shape=jax.ShapeDtypeStruct((cols, rows) +...]
    all_gather x1 -> x0, blocking collectives: 14.2 us -> none  [local_split(): lax.all_gather(mod_part, ('row', 'col'), axis=0, tiled=True)]
    unnamed x101 -> x93, local copies, waits for them, and re-layouts: 29.1 us -> 42.2 us
    pallas_call x7, Pallas kernels: 78.2 us -> 85.9 us  [exchange_rows(): pl.pallas_call(exchange_body, out_shape=jax.ShapeDtypeStruct(value.shape,...]
where the time goes in v3:
time: 748 us; the launch traced here: 735 us
  Pallas kernels  448 us (60%)
  local copies, waits for them, and re-layouts  105 us (14%)
  waiting for transfers between devices  83.7 us (11%)
  other arithmetic  44.7 us (6%)
  matrix products  42.2 us (6%)
  starting transfers between devices  9.78 us (1%)
    pallas_call x8, Pallas kernels, gather_tokens(): pl.pallas_call(gather_body, out_shape=jax.ShapeDtypeStruct((cols, rows) +...  244 us
    pallas_call x7, Pallas kernels, block_call(): pl.pallas_call(block_body, grid_spec=grid_spec, out_shape=[jax.ShapeDtype...  114 us
    pallas_call x7, Pallas kernels, exchange_rows(): pl.pallas_call(exchange_body, out_shape=jax.ShapeDtypeStruct(value.shape,...  85.9 us
    ppermute x6, waiting for transfers between devices, passed_along(): return lax.ppermute(value, axis, pairs)  71.4 us
    unnamed x93, local copies, waits for them, and re-layouts  42.2 us
    dot_general x7, matrix products, local_split(): jnp.dot(returned, out_weight[0], preferred_element_type=jnp.float32)  36.4 us
  transfers between devices with their start and end apart: 13, of which 13 were waited for; matrix products, arithmetic and copies ran while one was open for 0% of the time, Pallas kernels for 0%

profile of v3, /device:TPU:6, one launch (start us, length us, event | category | flops | bytes accessed | tf_op | source)
XLA Modules:
  0.0 735.1 jit_solution(14328115176101379741)
XLA Ops:
  21.3 12.3 %shard_map.109 = f32[2,4,1,8,2304]{4,3,2,1,0:T(8,128)} custom-call(f32[1,8,2304]{2,1,0:T(8,128)} %broadcast_in_dim.322.x_ref), custom_call_target="tpu_custom_call" | custom-call | bytes 41943040 | tf_op jit(solution)/shard_map/pallas_call | solution.py:411
  39.4 45.0 %shard_map.110 = bf16[2,4,3,32,3072]{4,3,2,1,0:T(8,128)(2,1)} custom-call(bf16[3,32,3072]{2,1,0:T(8,128)(2,1)} %pad_maximum_fusion.3.x_ref), custom_call_target="tpu_custom_call" | custom-call | bytes 41943040 | tf_op jit(solution)/shard_map/pallas_call | solution.py:411
  154.6 16.2 %shard_map.112 = (bf16[2,6,4,256,128]{4,3,2,1,0:T(8,128)(2,1)S(1)}, bf16[4,2,2,32,384]{4,3,2,1,0:T(8,128)(2,1)S(1)}) custom-call(s32[1]{0:T(128)} %bitcast.8.patch_ref, s32[1]{0:T(128)} %bitcast.9.cell_ref, bf16[2,4,2,32,3072]{4,3,2,1,0:T(8,128)(2,1)S(1)} %copy-done.3, bf16[1,3072,4608]{2,1,0:T(8,128)(2,1)} %w_ref.15, ...), custom_call_target="tpu_custom_call" | custom-call | flops 5234491392 | bytes 20971520 | tf_op jit(solution)/shard_map/pallas_call | solution.py:316
  211.5 30.7 %shard_map.114.x_ref = bf16[2,4,2,32,3072]{4,3,2,1,0:T(8,128)(2,1)} custom-call(bf16[2,32,3072]{2,1,0:T(8,128)(2,1)} %fusion.79.x_ref), custom_call_target="tpu_custom_call" | custom-call | bytes 41943040 | tf_op jit(solution)/shard_map/pallas_call | solution.py:411
  244.1 16.2 %shard_map.115 = (bf16[2,6,4,256,128]{4,3,2,1,0:T(8,128)(2,1)S(1)}, bf16[4,2,2,32,384]{4,3,2,1,0:T(8,128)(2,1)S(1)}) custom-call(s32[1]{0:T(128)} %bitcast.68.patch_ref, s32[1]{0:T(128)} %bitcast.9.cell_ref, bf16[2,4,2,32,3072]{4,3,2,1,0:T(8,128)(2,1)S(1)} %copy-done.5, bf16[1,3072,4608]{2,1,0:T(8,128)(2,1)} %w_ref.15, ...), custom_call_target="tpu_custom_call" | custom-call | flops 5234491392 | bytes 20971520 | tf_op jit(solution)/shard_map/pallas_call | solution.py:316
  299.4 31.2 %shard_map.117.x_ref = bf16[2,4,2,32,3072]{4,3,2,1,0:T(8,128)(2,1)} custom-call(bf16[2,32,3072]{2,1,0:T(8,128)(2,1)} %fusion.75.x_ref), custom_call_target="tpu_custom_call" | custom-call | bytes 41943040 | tf_op jit(solution)/shard_map/pallas_call | solution.py:411
  332.4 16.2 %shard_map.118 = (bf16[2,6,4,256,128]{4,3,2,1,0:T(8,128)(2,1)S(1)}, bf16[4,2,2,32,384]{4,3,2,1,0:T(8,128)(2,1)S(1)}) custom-call(s32[1]{0:T(128)} %bitcast.76.patch_ref, s32[1]{0:T(128)} %bitcast.9.cell_ref, bf16[2,4,2,32,3072]{4,3,2,1,0:T(8,128)(2,1)S(1)} %copy-done.6, bf16[1,3072,4608]{2,1,0:T(8,128)(2,1)} %w_ref.15, ...), custom_call_target="tpu_custom_call" | custom-call | flops 5234491392 | bytes 20971520 | tf_op jit(solution)/shard_map/pallas_call | solution.py:316
  351.1 12.1 %shard_map.119 = bf16[4,2,2,32,384]{4,3,2,1,0:T(8,128)(2,1)} custom-call(bf16[4,2,2,32,384]{4,3,2,1,0:T(8,128)(2,1)} %copy-done.19), custom_call_target="tpu_custom_call" | custom-call | bytes 16777216 | tf_op jit(solution)/shard_map/pallas_call | solution.py:479
  374.2 12.1 %collective-permute-done.5 = bf16[2,32,3072]{2,1,0:T(8,128)(2,1)S(1)} collective-permute-done((bf16[2,32,3072]{2,1,0:T(8,128)(2,1)S(1)}, bf16[2,32,3072]{2,1,0:T(8,128)(2,1)S(1)}, u32[]{:S(2)}, u32[]{:S(2)}) %collective-permute-start.5) | collective-permute-done | bytes 393248 | tf_op jit(solution)/shard_map/ppermute | solution.py:18
  388.8 31.3 %shard_map.120.x_ref = bf16[2,4,2,32,3072]{4,3,2,1,0:T(8,128)(2,1)} custom-call(bf16[2,32,3072]{2,1,0:T(8,128)(2,1)} %fusion.71.x_ref), custom_call_target="tpu_custom_call" | custom-call | bytes 41943040 | tf_op jit(solution)/shard_map/pallas_call | solution.py:411
  422.0 16.2 %shard_map.121 = (bf16[2,6,4,256,128]{4,3,2,1,0:T(8,128)(2,1)S(1)}, bf16[4,2,2,32,384]{4,3,2,1,0:T(8,128)(2,1)S(1)}) custom-call(s32[1]{0:T(128)} %bitcast.84.patch_ref, s32[1]{0:T(128)} %bitcast.9.cell_ref, bf16[2,4,2,32,3072]{4,3,2,1,0:T(8,128)(2,1)S(1)} %copy-done.7, bf16[1,3072,4608]{2,1,0:T(8,128)(2,1)} %w_ref.15, ...), custom_call_target="tpu_custom_call" | custom-call | flops 5234491392 | bytes 20971520 | tf_op jit(solution)/shard_map/pallas_call | solution.py:316
  440.6 12.8 %shard_map.122 = bf16[4,2,2,32,384]{4,3,2,1,0:T(8,128)(2,1)} custom-call(bf16[4,2,2,32,384]{4,3,2,1,0:T(8,128)(2,1)} %copy-done.20), custom_call_target="tpu_custom_call" | custom-call | bytes 16777216 | tf_op jit(solution)/shard_map/pallas_call | solution.py:479
  464.3 12.1 %collective-permute-done.7 = bf16[2,32,3072]{2,1,0:T(8,128)(2,1)S(1)} collective-permute-done((bf16[2,32,3072]{2,1,0:T(8,128)(2,1)S(1)}, bf16[2,32,3072]{2,1,0:T(8,128)(2,1)S(1)}, u32[]{:S(2)}, u32[]{:S(2)}) %collective-permute-start.7) | collective-permute-done | bytes 393248 | tf_op jit(solution)/shard_map/ppermute | solution.py:18
  477.9 31.2 %shard_map.123.x_ref = bf16[2,4,2,32,3072]{4,3,2,1,0:T(8,128)(2,1)} custom-call(bf16[2,32,3072]{2,1,0:T(8,128)(2,1)} %fusion.67.x_ref), custom_call_target="tpu_custom_call" | custom-call | bytes 41943040 | tf_op jit(solution)/shard_map/pallas_call | solution.py:411
  511.0 16.2 %shard_map.124 = (bf16[2,6,4,256,128]{4,3,2,1,0:T(8,128)(2,1)S(1)}, bf16[4,2,2,32,384]{4,3,2,1,0:T(8,128)(2,1)S(1)}) custom-call(s32[1]{0:T(128)} %bitcast.91.patch_ref, s32[1]{0:T(128)} %bitcast.9.cell_ref, bf16[2,4,2,32,3072]{4,3,2,1,0:T(8,128)(2,1)S(1)} %copy-done.8, bf16[1,3072,4608]{2,1,0:T(8,128)(2,1)} %w_ref.15, ...), custom_call_target="tpu_custom_call" | custom-call | flops 5234491392 | bytes 20971520 | tf_op jit(solution)/shard_map/pallas_call | solution.py:316
  529.7 12.8 %shard_map.125 = bf16[4,2,2,32,384]{4,3,2,1,0:T(8,128)(2,1)} custom-call(bf16[4,2,2,32,384]{4,3,2,1,0:T(8,128)(2,1)} %copy-done.21), custom_call_target="tpu_custom_call" | custom-call | bytes 16777216 | tf_op jit(solution)/shard_map/pallas_call | solution.py:479
  553.5 12.0 %collective-permute-done.9 = bf16[2,32,3072]{2,1,0:T(8,128)(2,1)S(1)} collective-permute-done((bf16[2,32,3072]{2,1,0:T(8,128)(2,1)S(1)}, bf16[2,32,3072]{2,1,0:T(8,128)(2,1)S(1)}, u32[]{:S(2)}, u32[]{:S(2)}) %collective-permute-start.9) | collective-permute-done | bytes 393248 | tf_op jit(solution)/shard_map/ppermute | solution.py:18
  567.0 31.2 %shard_map.126.x_ref = bf16[2,4,2,32,3072]{4,3,2,1,0:T(8,128)(2,1)} custom-call(bf16[2,32,3072]{2,1,0:T(8,128)(2,1)} %fusion.63.x_ref), custom_call_target="tpu_custom_call" | custom-call | bytes 41943040 | tf_op jit(solution)/shard_map/pallas_call | solution.py:411
  600.1 16.2 %shard_map.127 = (bf16[2,6,4,256,128]{4,3,2,1,0:T(8,128)(2,1)S(1)}, bf16[4,2,2,32,384]{4,3,2,1,0:T(8,128)(2,1)S(1)}) custom-call(s32[1]{0:T(128)} %bitcast.98.patch_ref, s32[1]{0:T(128)} %bitcast.9.cell_ref, bf16[2,4,2,32,3072]{4,3,2,1,0:T(8,128)(2,1)S(1)} %copy-done.9, bf16[1,3072,4608]{2,1,0:T(8,128)(2,1)} %w_ref.15, ...), custom_call_target="tpu_custom_call" | custom-call | flops 5234491392 | bytes 20971520 | tf_op jit(solution)/shard_map/pallas_call | solution.py:316
  618.8 12.8 %shard_map.128 = bf16[4,2,2,32,384]{4,3,2,1,0:T(8,128)(2,1)} custom-call(bf16[4,2,2,32,384]{4,3,2,1,0:T(8,128)(2,1)} %copy-done.22), custom_call_target="tpu_custom_call" | custom-call | bytes 16777216 | tf_op jit(solution)/shard_map/pallas_call | solution.py:479
  642.6 12.0 %collective-permute-done.11 = bf16[2,32,3072]{2,1,0:T(8,128)(2,1)S(1)} collective-permute-done((bf16[2,32,3072]{2,1,0:T(8,128)(2,1)S(1)}, bf16[2,32,3072]{2,1,0:T(8,128)(2,1)S(1)}, u32[]{:S(2)}, u32[]{:S(2)}) %collective-permute-start.11) | collective-permute-done | bytes 393248 | tf_op jit(solution)/shard_map/ppermute | solution.py:18
  656.1 31.3 %shard_map.129.x_ref = bf16[2,4,2,32,3072]{4,3,2,1,0:T(8,128)(2,1)} custom-call(bf16[2,32,3072]{2,1,0:T(8,128)(2,1)} %fusion.59.x_ref), custom_call_target="tpu_custom_call" | custom-call | bytes 41943040 | tf_op jit(solution)/shard_map/pallas_call | solution.py:411
  689.2 17.0 %shard_map.130 = (bf16[2,6,4,256,128]{4,3,2,1,0:T(8,128)(2,1)}, bf16[4,2,2,32,384]{4,3,2,1,0:T(8,128)(2,1)S(1)}) custom-call(s32[1]{0:T(128)} %bitcast.105.patch_ref, s32[1]{0:T(128)} %bitcast.9.cell_ref, bf16[2,4,2,32,3072]{4,3,2,1,0:T(8,128)(2,1)S(1)} %copy-done.4, bf16[1,3072,4608]{2,1,0:T(8,128)(2,1)} %w_ref.15, ...), custom_call_target="tpu_custom_call" | custom-call | flops 5234491392 | bytes 20971520 | tf_op jit(solution)/shard_map/pallas_call | solution.py:316
  707.0 12.8 %shard_map.131 = bf16[4,2,2,32,384]{4,3,2,1,0:T(8,128)(2,1)} custom-call(bf16[4,2,2,32,384]{4,3,2,1,0:T(8,128)(2,1)} %copy-done.16), custom_call_target="tpu_custom_call" | custom-call | bytes 16777216 | tf_op jit(solution)/shard_map/pallas_call | solution.py:479
  (296 shorter events, 262.6 us)
Async XLA Ops:
  0.0 19.5 %copy-start = (bf16[1,512,2304]{2,1,0:T(8,128)(2,1)S(1)}, bf16[1,512,2304]{2,1,0:T(8,128)(2,1)}, u32[]{:S(2)}) copy-start(bf16[1,512,2304]{2,1,0:T(8,128)(2,1)} %param.15) | copy-start | bytes 7077892
  0.0 18.6 %copy-start.31 = (s32[2,96]{1,0:T(2,128)S(1)}, s32[2,96]{1,0:T(2,128)}, u32[]{:S(2)}) copy-start(s32[2,96]{1,0:T(2,128)} %param.21) | copy-start | bytes 2308
  16.8 18.4 %copy-start.24 = (f32[24,3072]{1,0:T(8,128)S(1)}, f32[24,3072]{1,0:T(8,128)}, u32[]{:S(2)}) copy-start(f32[24,3072]{1,0:T(8,128)} %reshape.835) | copy-start | bytes 884740
  34.9 605.1 %copy-start.25 = (f32[1,3072]{1,0:T(1,128)}, f32[1,3072]{1,0:T(1,128)S(1)}, u32[]{:S(2)}) copy-start(f32[1,3072]{1,0:T(1,128)S(1)} %get-tuple-element.62) | copy-start | bytes 36868
  37.1 47.2 %copy-start.23 = (bf16[4,32,2,3072]{3,1,2,0:T(8,128)(2,1)}, bf16[4,32,2,3072]{3,1,2,0:T(8,128)(2,1)S(1)}, u32[]{:S(2)}) copy-start(bf16[4,32,2,3072]{3,1,2,0:T(8,128)(2,1)S(1)} %copy.108) | copy-start | bytes 4718596
  102.0 10.1 %copy-start.30 = (s32[2,4,2,12]{3,2,1,0:T(2,128)S(1)}, s32[2,4,2,12]{3,2,1,0:T(2,128)}, u32[]{:S(2)}) copy-start(s32[2,4,2,12]{3,2,1,0:T(2,128)} %reshape.808) | copy-start | bytes 2308
  102.0 10.5 %copy-start.29 = (pred[4,2,4,2,32]{4,3,2,1,0:T(4,128)(4,1)S(1)}, pred[4,2,4,2,32]{4,3,2,1,0:T(4,128)(4,1)}, u32[]{:S(2)}) copy-start(pred[4,2,4,2,32]{4,3,2,1,0:T(4,128)(4,1)} %get-tuple-element.65) | copy-start | bytes 6148
  102.0 10.6 %copy-start.28 = (pred[4,2,4,2,32]{4,3,2,1,0:T(4,128)(4,1)S(1)}, pred[4,2,4,2,32]{4,3,2,1,0:T(4,128)(4,1)}, u32[]{:S(2)}) copy-start(pred[4,2,4,2,32]{4,3,2,1,0:T(4,128)(4,1)} %get-tuple-element.66) | copy-start | bytes 6148
  102.0 11.1 %copy-start.27 = (s32[1024,2]{1,0:T(8,128)S(1)}, s32[1024,2]{1,0:T(8,128)}, u32[]{:S(2)}) copy-start(s32[1024,2]{1,0:T(8,128)} %gather_fusion.1) | copy-start | bytes 24580
  102.1 13.0 %copy-start.34 = (f32[8]{0:T(128)S(1)}, f32[8]{0:T(128)}, u32[]{:S(2)}) copy-start(f32[8]{0:T(128)} %negate_power_fusion.1) | copy-start | bytes 100
  102.1 13.2 %copy-start.32 = (f32[12]{0:T(128)S(1)}, f32[12]{0:T(128)}, u32[]{:S(2)}) copy-start(f32[12]{0:T(128)} %negate_power_fusion) | copy-start | bytes 148
  191.7 1.9 collective-permute-start
  195.7 13.2 %collective-permute-start.1 = (bf16[2,32,3072]{2,1,0:T(8,128)(2,1)}, bf16[2,32,3072]{2,1,0:T(8,128)(2,1)S(1)}, u32[]{:S(2)}, u32[]{:S(2)}) collective-permute-start(bf16[2,32,3072]{2,1,0:T(8,128)(2,1)} %get-tuple-element.48), channel_id=1, source_target_pairs={{0,8},{8,16},{16,24},{1,9},{9,17},{17,25},{2,10},{10,18},{18,26},{... | collective-permute-start | bytes 1179656 | tf_op jit(solution)/shard_map/ppermute | solution.py:18
  281.0 1.8 collective-permute-start.2
  283.8 13.0 %collective-permute-start.3 = (bf16[2,32,3072]{2,1,0:T(8,128)(2,1)S(1)}, bf16[2,32,3072]{2,1,0:T(8,128)(2,1)S(1)}, u32[]{:S(2)}, u32[]{:S(2)}) collective-permute-start(bf16[2,32,3072]{2,1,0:T(8,128)(2,1)S(1)} %get-tuple-element.44), channel_id=1, source_target_pairs={{0,8},{8,16},{16,24},{1,9},{9,17},{17,25},{2,10},{10,18},{18,26},{... | collective-permute-start | bytes 1179656 | tf_op jit(solution)/shard_map/ppermute | solution.py:18
  369.9 1.8 collective-permute-start.4
  372.7 13.6 %collective-permute-start.5 = (bf16[2,32,3072]{2,1,0:T(8,128)(2,1)S(1)}, bf16[2,32,3072]{2,1,0:T(8,128)(2,1)S(1)}, u32[]{:S(2)}, u32[]{:S(2)}) collective-permute-start(bf16[2,32,3072]{2,1,0:T(8,128)(2,1)S(1)} %get-tuple-element.40), channel_id=1, source_target_pairs={{0,8},{8,16},{16,24},{1,9},{9,17},{17,25},{2,10},{10,18},{18,26},{... | collective-permute-start | bytes 1179656 | tf_op jit(solution)/shard_map/ppermute | solution.py:18
  460.0 1.8 collective-permute-start.6
  462.8 13.6 %collective-permute-start.7 = (bf16[2,32,3072]{2,1,0:T(8,128)(2,1)S(1)}, bf16[2,32,3072]{2,1,0:T(8,128)(2,1)S(1)}, u32[]{:S(2)}, u32[]{:S(2)}) collective-permute-start(bf16[2,32,3072]{2,1,0:T(8,128)(2,1)S(1)} %get-tuple-element.36), channel_id=1, source_target_pairs={{0,8},{8,16},{16,24},{1,9},{9,17},{17,25},{2,10},{10,18},{18,26},{... | collective-permute-start | bytes 1179656 | tf_op jit(solution)/shard_map/ppermute | solution.py:18
  549.1 1.8 collective-permute-start.8
  551.9 13.6 %collective-permute-start.9 = (bf16[2,32,3072]{2,1,0:T(8,128)(2,1)S(1)}, bf16[2,32,3072]{2,1,0:T(8,128)(2,1)S(1)}, u32[]{:S(2)}, u32[]{:S(2)}) collective-permute-start(bf16[2,32,3072]{2,1,0:T(8,128)(2,1)S(1)} %get-tuple-element.34), channel_id=1, source_target_pairs={{0,8},{8,16},{16,24},{1,9},{9,17},{17,25},{2,10},{10,18},{18,26},{... | collective-permute-start | bytes 1179656 | tf_op jit(solution)/shard_map/ppermute | solution.py:18
  638.2 1.8 collective-permute-start.10
  641.0 13.6 %collective-permute-start.11 = (bf16[2,32,3072]{2,1,0:T(8,128)(2,1)S(1)}, bf16[2,32,3072]{2,1,0:T(8,128)(2,1)S(1)}, u32[]{:S(2)}, u32[]{:S(2)}) collective-permute-start(bf16[2,32,3072]{2,1,0:T(8,128)(2,1)S(1)} %get-tuple-element.32), channel_id=1, source_target_pairs={{0,8},{8,16},{16,24},{1,9},{9,17},{17,25},{2,10},{10,18},{18,26},{... | collective-permute-start | bytes 1179656 | tf_op jit(solution)/shard_map/ppermute | solution.py:18
  726.2 1.9 collective-permute-start.12
  (29 other events, 95.6 us)
